TPU v7x, 32 devices: a whole 2x2x4 slice. The times are simulated.
32 devices in a mesh: batch: 8 (over z, y), band: 4 (over x, core).
Axes of the slice: x: 2, y: 2, z: 4, core: 2. Of those that a mesh axis runs over, the one named last changes fastest.
Arguments:
- patches: bfloat16 [64, 256, 768], P('batch', 'band'), may hold values from -6 to 6
- queries: bfloat16 [64, 256, 768], P('batch', 'band'), may hold values from -6 to 6
- cotangent: bfloat16 [64, 256, 768], P('batch', 'band'), may hold values from -6 to 6
- counts: int32 [64], P('batch'), may hold values from 16 to 256, as said below
- masked: int32 [64, 256], P('batch', 'band'), may hold values from 0 to 1, as said below
- enc_gains: float32 [2, 768], replicated, may hold values from 0.5 to 1.5
- enc_shifts: float32 [6, 768], replicated, may hold values from -3 to 3
- enc_widebias: float32 [3072], replicated, may hold values from -3 to 3
- enc_scales: float32 [2, 768], replicated, may hold values from 0.5 to 1.5
- enc_project: bfloat16 [768, 2304], replicated, may hold values from -0.21875 to 0.21875
- enc_output: bfloat16 [768, 768], replicated, may hold values from -0.625 to 0.625
- enc_expand: bfloat16 [768, 3072], replicated, may hold values from -0.21875 to 0.21875
- enc_reduce: bfloat16 [3072, 768], replicated, may hold values from -0.109375 to 0.109375
- reg_gains: float32 [3, 768], replicated, may hold values from 0.5 to 1.5
- reg_shifts: float32 [7, 768], replicated, may hold values from -3 to 3
- reg_widebias: float32 [3072], replicated, may hold values from -3 to 3
- reg_scales: float32 [2, 768], replicated, may hold values from 0.5 to 1.5
- reg_query: bfloat16 [768, 768], replicated, may hold values from -0.21875 to 0.21875
- reg_keyval: bfloat16 [768, 1536], replicated, may hold values from -0.21875 to 0.21875
- reg_output: bfloat16 [768, 768], replicated, may hold values from -0.625 to 0.625
- reg_expand: bfloat16 [768, 3072], replicated, may hold values from -0.21875 to 0.21875
- reg_reduce: bfloat16 [3072, 768], replicated, may hold values from -0.109375 to 0.109375
Outputs:
- prediction: float32 [64, 256, 768], P('batch', 'band')
- patch_grad: float32 [64, 256, 768], P('batch', 'band')
- query_grad: float32 [64, 256, 768], P('batch', 'band')
- enc_gains_grad: float32 [2, 768], P(None, 'band')
- enc_shifts_grad: float32 [6, 768], P(None, 'band')
- enc_wide_grad: float32 [3072], P('band')
- enc_scales_grad: float32 [2, 768], P(None, 'band')
- enc_project_grad: float32 [768, 2304], P('band')
- enc_output_grad: float32 [768, 768], P('band')
- enc_expand_grad: float32 [768, 3072], P('band')
- enc_reduce_grad: float32 [3072, 768], P('band')
- reg_gains_grad: float32 [3, 768], P(None, 'band')
- reg_shifts_grad: float32 [7, 768], P(None, 'band')
- reg_wide_grad: float32 [3072], P('band')
- reg_scales_grad: float32 [2, 768], P(None, 'band')
- reg_query_grad: float32 [768, 768], P('band')
- reg_keyval_grad: float32 [768, 1536], P('band')
- reg_output_grad: float32 [768, 768], P('band')
- reg_expand_grad: float32 [768, 3072], P('band')
- reg_reduce_grad: float32 [3072, 768], P('band')
Inputs may be any that keep to these rules, and one draw needn't show every extreme that they name: Slot p of image i is real when p < counts[i]; some image has all 256 slots real. 1 marks a masked slot; slot 0 of every image is never masked.
All inputs are finite; a program needn't handle non-finite values.
Results may differ from a plain program's by a relative error of at most 0.03.
Values may be sent and summed in bfloat16 or wider, within the bound.
No kernel may reach another device: no remote copies, remote signals or barrier semaphores. Data moves between devices by JAX's collectives and lax.ppermute only.
A program may use at most 256 MiB of HBM per device.

v0:
```python
import jax
import jax.numpy as jnp
from jax import lax
from jax.sharding import PartitionSpec as P

HEADS = 12
HD = 64


EPS = 1e-06
ROOT_HALF = 0.7071067811865476
INV_ROOT_TAU = 0.3989422804014327
NEG_LARGE = -1e30


def normalize(values, norm_gain, norm_shift):
    row_mean = jnp.mean(values, -1, keepdims=True)
    centred = values - row_mean
    variance = jnp.mean(centred * centred, -1, keepdims=True)
    inv_std = lax.rsqrt(variance + EPS)
    unit_rows = centred * inv_std
    return (unit_rows * norm_gain + norm_shift, unit_rows, inv_std)


def normalize_back(grad_out, unit_rows, inv_std, norm_gain):
    scaled = grad_out * norm_gain
    first_term = jnp.mean(scaled, -1, keepdims=True)
    second_term = jnp.mean(scaled * unit_rows, -1, keepdims=True)
    grad_in = inv_std * (scaled - first_term - unit_rows * second_term)
    return (grad_in, jnp.sum(grad_out * unit_rows, (0, 1)), jnp.sum(grad_out, (0, 1)))


def smooth_gate(pre_act):
    return 0.5 * pre_act * (1.0 + lax.erf(pre_act * ROOT_HALF))


def gate_slope(pre_act):
    return 0.5 * (1.0 + lax.erf(pre_act * ROOT_HALF)) + pre_act * INV_ROOT_TAU * jnp.exp(
        -0.5 * pre_act * pre_act
    )


def apply_weight(row_data, weight):
    return jnp.einsum("nsi,ij->nsj", row_data, weight, preferred_element_type=jnp.float32)


def apply_back(grad_rows, weight):
    return jnp.einsum("nsj,ij->nsi", grad_rows, weight, preferred_element_type=jnp.float32)


def weight_grad(row_data, grad_rows):
    return jnp.einsum("nsi,nsj->ij", row_data, grad_rows, preferred_element_type=jnp.float32)


def column_sum(grad_rows):
    return jnp.sum(grad_rows.astype(jnp.float32), (0, 1))


def split_heads(row_data):
    return row_data.reshape(row_data.shape[0], row_data.shape[1], HEADS, -1)


def masked_scores(query_low, key_low, keep_img):
    raw_scores = jnp.einsum(
        "nqhd,nkhd->nhqk",
        split_heads(query_low),
        split_heads(key_low),
        preferred_element_type=jnp.float32,
    ) * HD ** (-0.5)
    return jnp.where(keep_img[:, None, None, :] > 0, raw_scores, NEG_LARGE)


def attend_forward(query_low, key_low, value_low, keep_img):
    scores = masked_scores(query_low, key_low, keep_img)
    row_top = jnp.max(scores, -1, keepdims=True)
    exp_scores = jnp.exp(scores - row_top)
    row_total = jnp.sum(exp_scores, -1, keepdims=True)
    weights_low = (exp_scores / row_total).astype(jnp.bfloat16)
    mixed = jnp.einsum(
        "nhqk,nkhd->nqhd", weights_low, split_heads(value_low), preferred_element_type=jnp.float32
    )
    return (mixed.reshape(query_low.shape), row_top + jnp.log(row_total))


def attend_backward(query_low, key_low, value_low, keep_img, log_total, grad_mixed):
    scores = masked_scores(query_low, key_low, keep_img)
    probs_full = jnp.exp(scores - log_total)
    probs_low = probs_full.astype(jnp.bfloat16)
    grad_heads = split_heads(grad_mixed)
    grad_value = jnp.einsum(
        "nhqk,nqhd->nkhd", probs_low, grad_heads, preferred_element_type=jnp.float32
    )
    grad_probs = jnp.einsum(
        "nqhd,nkhd->nhqk", grad_heads, split_heads(value_low), preferred_element_type=jnp.float32
    )
    inner_sum = jnp.sum(grad_probs * probs_full, -1, keepdims=True)
    grad_scores = (probs_full * (grad_probs - inner_sum)).astype(jnp.bfloat16)
    grad_query = jnp.einsum(
        "nhqk,nkhd->nqhd", grad_scores, split_heads(key_low), preferred_element_type=jnp.float32
    ) * HD ** (-0.5)
    grad_key = jnp.einsum(
        "nhqk,nqhd->nkhd", grad_scores, split_heads(query_low), preferred_element_type=jnp.float32
    ) * HD ** (-0.5)
    full_shape = query_low.shape
    return (
        grad_query.reshape(full_shape),
        grad_key.reshape(full_shape),
        grad_value.reshape(full_shape),
    )


def mlp_forward(middle, norm_gain, norm_shift, expand, wide_bias, reduce_weight, out_bias):
    normed, unit_rows, inv_std = normalize(middle, norm_gain, norm_shift)
    normed_low = normed.astype(jnp.bfloat16)
    pre_act = apply_weight(normed_low, expand) + wide_bias
    act_low = smooth_gate(pre_act).astype(jnp.bfloat16)
    result = apply_weight(act_low, reduce_weight) + out_bias
    return (result, (normed_low, unit_rows, inv_std, pre_act, act_low))


def mlp_backward(grad_result, mlp_cache, norm_gain, expand, reduce_weight):
    normed_low, unit_rows, inv_std, pre_act, act_low = mlp_cache
    grad_low = grad_result.astype(jnp.bfloat16)
    reduce_grad = weight_grad(act_low, grad_low)
    out_bias_grad = column_sum(grad_low)
    grad_act = apply_back(grad_low, reduce_weight)
    grad_pre = (grad_act * gate_slope(pre_act)).astype(jnp.bfloat16)
    wide_grad = column_sum(grad_pre)
    expand_grad = weight_grad(normed_low, grad_pre)
    grad_normed = apply_back(grad_pre, expand)
    grad_middle, gain_grad, shift_grad = normalize_back(grad_normed, unit_rows, inv_std, norm_gain)
    return (grad_middle, gain_grad, shift_grad, expand_grad, wide_grad, reduce_grad, out_bias_grad)


def body(
    patches,
    queries,
    cotangent,
    counts,
    masked,
    enc_gains,
    enc_shifts,
    enc_widebias,
    enc_scales,
    enc_project,
    enc_output,
    enc_expand,
    enc_reduce,
    reg_gains,
    reg_shifts,
    reg_widebias,
    reg_scales,
    reg_query,
    reg_keyval,
    reg_output,
    reg_expand,
    reg_reduce,
):
    model_width = patches.shape[2]
    band_rows = patches.shape[1]
    slot_index = lax.axis_index("band") * band_rows + jnp.arange(band_rows, dtype=jnp.int32)
    is_valid = slot_index[None, :] < counts[:, None]
    keep_band = jnp.where(is_valid & (masked == 0), 1.0, 0.0).astype(jnp.float32)
    pick_band = jnp.where(is_valid & (masked == 1), 1.0, 0.0).astype(jnp.float32)[:, :, None]
    blank_row = jnp.zeros((model_width,), jnp.float32)
    inputs = patches.astype(jnp.float32)
    enc_normed, enc_unit, enc_inv = normalize(inputs, enc_gains[0], enc_shifts[0])
    enc_rows, keep_low = (
        lax.all_to_all(
            enc_normed.astype(jnp.bfloat16), "band", split_axis=0, concat_axis=1, tiled=True
        ),
        lax.all_to_all(
            keep_band.astype(jnp.bfloat16), "band", split_axis=0, concat_axis=1, tiled=True
        ),
    )
    keep_img = keep_low.astype(jnp.float32)
    triple = (
        apply_weight(enc_rows, enc_project)
        + jnp.concatenate([enc_shifts[1], blank_row, enc_shifts[2]])
    ).astype(jnp.bfloat16)
    enc_query = triple[..., :model_width]
    enc_key = triple[..., model_width : 2 * model_width]
    enc_value = triple[..., 2 * model_width :]
    enc_mixed, enc_total = attend_forward(enc_query, enc_key, enc_value, keep_img)
    enc_mixed_low = enc_mixed.astype(jnp.bfloat16)
    enc_branch = (apply_weight(enc_mixed_low, enc_output) + enc_shifts[3]).astype(jnp.bfloat16)
    enc_branch_band = lax.all_to_all(
        enc_branch, "band", split_axis=1, concat_axis=0, tiled=True
    ).astype(jnp.float32)
    enc_middle = inputs + enc_scales[0] * enc_branch_band
    enc_ffn, enc_cache = mlp_forward(
        enc_middle, enc_gains[1], enc_shifts[4], enc_expand, enc_widebias, enc_reduce, enc_shifts[5]
    )
    encoded = enc_middle + enc_scales[1] * enc_ffn
    query_in = queries.astype(jnp.float32)
    query_normed, query_unit, query_inv = normalize(query_in, reg_gains[0], reg_shifts[0])
    pair_normed, pair_unit, pair_inv = normalize(encoded, reg_gains[1], reg_shifts[1])
    query_rows, pair_rows = (
        lax.all_to_all(
            query_normed.astype(jnp.bfloat16), "band", split_axis=0, concat_axis=1, tiled=True
        ),
        lax.all_to_all(
            pair_normed.astype(jnp.bfloat16), "band", split_axis=0, concat_axis=1, tiled=True
        ),
    )
    reg_query_low = (apply_weight(query_rows, reg_query) + reg_shifts[2]).astype(jnp.bfloat16)
    reg_pair_low = (
        apply_weight(pair_rows, reg_keyval) + jnp.concatenate([blank_row, reg_shifts[3]])
    ).astype(jnp.bfloat16)
    reg_key = reg_pair_low[..., :model_width]
    reg_value = reg_pair_low[..., model_width:]
    reg_mixed, reg_total = attend_forward(reg_query_low, reg_key, reg_value, keep_img)
    reg_mixed_low = reg_mixed.astype(jnp.bfloat16)
    reg_branch = (apply_weight(reg_mixed_low, reg_output) + reg_shifts[4]).astype(jnp.bfloat16)
    reg_branch_band = lax.all_to_all(
        reg_branch, "band", split_axis=1, concat_axis=0, tiled=True
    ).astype(jnp.float32)
    reg_middle = query_in + reg_scales[0] * reg_branch_band
    reg_ffn, reg_cache = mlp_forward(
        reg_middle, reg_gains[2], reg_shifts[5], reg_expand, reg_widebias, reg_reduce, reg_shifts[6]
    )
    final_rows = reg_middle + reg_scales[1] * reg_ffn
    prediction = final_rows * pick_band
    grad_final = cotangent.astype(jnp.float32) * pick_band
    reg_scale1 = jnp.sum(grad_final * reg_ffn, (0, 1))
    (
        reg_ffn_grad,
        reg_gain2,
        reg_shift5,
        reg_expand_grad,
        reg_wide_grad,
        reg_reduce_grad,
        reg_shift6,
    ) = mlp_backward(grad_final * reg_scales[1], reg_cache, reg_gains[2], reg_expand, reg_reduce)
    reg_grad_mid = grad_final + reg_ffn_grad
    reg_scale0 = jnp.sum(reg_grad_mid * reg_branch_band, (0, 1))
    reg_branch_grad = lax.all_to_all(
        (reg_grad_mid * reg_scales[0]).astype(jnp.bfloat16),
        "band",
        split_axis=0,
        concat_axis=1,
        tiled=True,
    )
    reg_output_grad = weight_grad(reg_mixed_low, reg_branch_grad)
    reg_shift4 = column_sum(reg_branch_grad)
    reg_mixed_grad = apply_back(reg_branch_grad, reg_output).astype(jnp.bfloat16)
    reg_query_part, reg_key_part, reg_value_part = attend_backward(
        reg_query_low, reg_key, reg_value, keep_img, reg_total, reg_mixed_grad
    )
    reg_query_back = reg_query_part.astype(jnp.bfloat16)
    reg_pair_back = jnp.concatenate([reg_key_part, reg_value_part], -1).astype(jnp.bfloat16)
    reg_query_grad = weight_grad(query_rows, reg_query_back)
    reg_keyval_grad = weight_grad(pair_rows, reg_pair_back)
    reg_shift2 = column_sum(reg_query_back)
    reg_shift3 = column_sum(reg_pair_back[..., model_width:])
    query_side, pair_side = (
        lax.all_to_all(
            apply_back(reg_query_back, reg_query).astype(jnp.bfloat16),
            "band",
            split_axis=1,
            concat_axis=0,
            tiled=True,
        ),
        lax.all_to_all(
            apply_back(reg_pair_back, reg_keyval).astype(jnp.bfloat16),
            "band",
            split_axis=1,
            concat_axis=0,
            tiled=True,
        ),
    )
    query_norm_grad, reg_gain0, reg_shift0 = normalize_back(
        query_side.astype(jnp.float32), query_unit, query_inv, reg_gains[0]
    )
    query_grad = reg_grad_mid + query_norm_grad
    encoded_grad, reg_gain1, reg_shift1 = normalize_back(
        pair_side.astype(jnp.float32), pair_unit, pair_inv, reg_gains[1]
    )
    reg_gains_grad = jnp.stack([reg_gain0, reg_gain1, reg_gain2])
    reg_shifts_grad = jnp.stack(
        [reg_shift0, reg_shift1, reg_shift2, reg_shift3, reg_shift4, reg_shift5, reg_shift6]
    )
    reg_scales_grad = jnp.stack([reg_scale0, reg_scale1])
    enc_scale1 = jnp.sum(encoded_grad * enc_ffn, (0, 1))
    (
        enc_ffn_grad,
        enc_gain1,
        enc_shift4,
        enc_expand_grad,
        enc_wide_grad,
        enc_reduce_grad,
        enc_shift5,
    ) = mlp_backward(encoded_grad * enc_scales[1], enc_cache, enc_gains[1], enc_expand, enc_reduce)
    enc_grad_mid = encoded_grad + enc_ffn_grad
    enc_scale0 = jnp.sum(enc_grad_mid * enc_branch_band, (0, 1))
    enc_branch_grad = lax.all_to_all(
        (enc_grad_mid * enc_scales[0]).astype(jnp.bfloat16),
        "band",
        split_axis=0,
        concat_axis=1,
        tiled=True,
    )
    enc_output_grad = weight_grad(enc_mixed_low, enc_branch_grad)
    enc_shift3 = column_sum(enc_branch_grad)
    enc_mixed_grad = apply_back(enc_branch_grad, enc_output).astype(jnp.bfloat16)
    enc_query_part, enc_key_part, enc_value_part = attend_backward(
        enc_query, enc_key, enc_value, keep_img, enc_total, enc_mixed_grad
    )
    triple_grad = jnp.concatenate([enc_query_part, enc_key_part, enc_value_part], -1).astype(
        jnp.bfloat16
    )
    enc_project_grad = weight_grad(enc_rows, triple_grad)
    enc_shift1 = column_sum(triple_grad[..., :model_width])
    enc_shift2 = column_sum(triple_grad[..., 2 * model_width :])
    enc_rows_grad = lax.all_to_all(
        apply_back(triple_grad, enc_project).astype(jnp.bfloat16),
        "band",
        split_axis=1,
        concat_axis=0,
        tiled=True,
    )
    patch_norm_grad, enc_gain0, enc_shift0 = normalize_back(
        enc_rows_grad.astype(jnp.float32), enc_unit, enc_inv, enc_gains[0]
    )
    patch_grad = enc_grad_mid + patch_norm_grad
    enc_gains_grad = jnp.stack([enc_gain0, enc_gain1])
    enc_shifts_grad = jnp.stack(
        [enc_shift0, enc_shift1, enc_shift2, enc_shift3, enc_shift4, enc_shift5]
    )
    enc_scales_grad = jnp.stack([enc_scale0, enc_scale1])
    (
        enc_gains_grad,
        enc_shifts_grad,
        enc_wide_grad,
        enc_scales_grad,
        enc_project_grad,
        enc_output_grad,
        enc_expand_grad,
        enc_reduce_grad,
        reg_gains_grad,
        reg_shifts_grad,
        reg_wide_grad,
        reg_scales_grad,
        reg_query_grad,
        reg_keyval_grad,
        reg_output_grad,
        reg_expand_grad,
        reg_reduce_grad,
    ) = (
        lax.psum_scatter(
            enc_gains_grad.astype(jnp.bfloat16), "band", scatter_dimension=1, tiled=True
        ).astype(jnp.float32),
        lax.psum_scatter(
            enc_shifts_grad.astype(jnp.bfloat16), "band", scatter_dimension=1, tiled=True
        ).astype(jnp.float32),
        lax.psum_scatter(
            enc_wide_grad.astype(jnp.bfloat16), "band", scatter_dimension=0, tiled=True
        ).astype(jnp.float32),
        lax.psum_scatter(
            enc_scales_grad.astype(jnp.bfloat16), "band", scatter_dimension=1, tiled=True
        ).astype(jnp.float32),
        lax.psum_scatter(
            enc_project_grad.astype(jnp.bfloat16), "band", scatter_dimension=0, tiled=True
        ).astype(jnp.float32),
        lax.psum_scatter(
            enc_output_grad.astype(jnp.bfloat16), "band", scatter_dimension=0, tiled=True
        ).astype(jnp.float32),
        lax.psum_scatter(
            enc_expand_grad.astype(jnp.bfloat16), "band", scatter_dimension=0, tiled=True
        ).astype(jnp.float32),
        lax.psum_scatter(
            enc_reduce_grad.astype(jnp.bfloat16), "band", scatter_dimension=0, tiled=True
        ).astype(jnp.float32),
        lax.psum_scatter(
            reg_gains_grad.astype(jnp.bfloat16), "band", scatter_dimension=1, tiled=True
        ).astype(jnp.float32),
        lax.psum_scatter(
            reg_shifts_grad.astype(jnp.bfloat16), "band", scatter_dimension=1, tiled=True
        ).astype(jnp.float32),
        lax.psum_scatter(
            reg_wide_grad.astype(jnp.bfloat16), "band", scatter_dimension=0, tiled=True
        ).astype(jnp.float32),
        lax.psum_scatter(
            reg_scales_grad.astype(jnp.bfloat16), "band", scatter_dimension=1, tiled=True
        ).astype(jnp.float32),
        lax.psum_scatter(
            reg_query_grad.astype(jnp.bfloat16), "band", scatter_dimension=0, tiled=True
        ).astype(jnp.float32),
        lax.psum_scatter(
            reg_keyval_grad.astype(jnp.bfloat16), "band", scatter_dimension=0, tiled=True
        ).astype(jnp.float32),
        lax.psum_scatter(
            reg_output_grad.astype(jnp.bfloat16), "band", scatter_dimension=0, tiled=True
        ).astype(jnp.float32),
        lax.psum_scatter(
            reg_expand_grad.astype(jnp.bfloat16), "band", scatter_dimension=0, tiled=True
        ).astype(jnp.float32),
        lax.psum_scatter(
            reg_reduce_grad.astype(jnp.bfloat16), "band", scatter_dimension=0, tiled=True
        ).astype(jnp.float32),
    )
    (
        enc_gains_grad,
        enc_shifts_grad,
        enc_wide_grad,
        enc_scales_grad,
        enc_project_grad,
        enc_output_grad,
        enc_expand_grad,
        enc_reduce_grad,
        reg_gains_grad,
        reg_shifts_grad,
        reg_wide_grad,
        reg_scales_grad,
        reg_query_grad,
        reg_keyval_grad,
        reg_output_grad,
        reg_expand_grad,
        reg_reduce_grad,
    ) = lax.psum(
        (
            enc_gains_grad,
            enc_shifts_grad,
            enc_wide_grad,
            enc_scales_grad,
            enc_project_grad,
            enc_output_grad,
            enc_expand_grad,
            enc_reduce_grad,
            reg_gains_grad,
            reg_shifts_grad,
            reg_wide_grad,
            reg_scales_grad,
            reg_query_grad,
            reg_keyval_grad,
            reg_output_grad,
            reg_expand_grad,
            reg_reduce_grad,
        ),
        "batch",
    )
    return (
        prediction,
        patch_grad,
        query_grad,
        enc_gains_grad,
        enc_shifts_grad,
        enc_wide_grad,
        enc_scales_grad,
        enc_project_grad,
        enc_output_grad,
        enc_expand_grad,
        enc_reduce_grad,
        reg_gains_grad,
        reg_shifts_grad,
        reg_wide_grad,
        reg_scales_grad,
        reg_query_grad,
        reg_keyval_grad,
        reg_output_grad,
        reg_expand_grad,
        reg_reduce_grad,
    )


def solution(mesh):
    in_specs = (
        P("batch", "band", None),
        P("batch", "band", None),
        P("batch", "band", None),
        P("batch"),
        P("batch", "band"),
        P(),
        P(),
        P(),
        P(),
        P(),
        P(),
        P(),
        P(),
        P(),
        P(),
        P(),
        P(),
        P(),
        P(),
        P(),
        P(),
        P(),
    )
    out_specs = (
        P("batch", "band", None),
        P("batch", "band", None),
        P("batch", "band", None),
        P(None, "band"),
        P(None, "band"),
        P("band"),
        P(None, "band"),
        P("band", None),
        P("band", None),
        P("band", None),
        P("band", None),
        P(None, "band"),
        P(None, "band"),
        P("band"),
        P(None, "band"),
        P("band", None),
        P("band", None),
        P("band", None),
        P("band", None),
        P("band", None),
    )
    return jax.shard_map(body, mesh=mesh, in_specs=in_specs, out_specs=out_specs, check_vma=False)
```

profile of v0, /device:TPU:0, one launch (start us, length us, event | category | flops | bytes accessed | tf_op | source)
XLA Modules:
  0.0 1369.5 jit_solution(11893629555120033341)
XLA Ops:
  29.5 6.9 all-to-all-done
  65.9 7.3 all-to-all-done.2
  82.1 7.3 multiply_convert_fusion.3
  137.2 10.3 all-to-all-done.5
  157.3 7.8 fusion.116
  181.7 10.3 all-to-all-done.6
  203.8 7.3 multiply_reduce_fusion.1
  257.8 7.1 fusion.115
  299.8 7.0 multiply_reduce_fusion
  393.3 7.4 bitcast_convert_fusion.1
  400.9 7.1 bitcast_convert_fusion
  408.1 7.0 bitcast_convert_fusion.2
  415.1 7.4 bitcast_convert_fusion.3
  428.1 12.9 all-reduce.4
  459.8 17.5 %reduce-scatter.40.cloned.1.call-done = bf16[192,768]{1,0:T(8,128)(2,1)} async-done(((bf16[768,768]{1,0:T(8,128)(2,1)}), bf16[192,768]{1,0:T(8,128)(2,1)}) %reduce-scatter.40.cloned.1.call-update) | async-done | bytes 294928 | tf_op jit(solution)/shard_map/reduce_scatter | solution.py:392
  477.3 28.5 %reduce-scatter.36.cloned.1.call-done = bf16[192,768]{1,0:T(8,128)(2,1)} async-done(((bf16[768,768]{1,0:T(8,128)(2,1)}), bf16[192,768]{1,0:T(8,128)(2,1)}) %reduce-scatter.36.cloned.1.call-update) | async-done | bytes 294928 | tf_op jit(solution)/shard_map/reduce_scatter | solution.py:386
  505.8 28.9 %reduce-scatter.30.cloned.1.call-done = bf16[192,768]{1,0:T(8,128)(2,1)} async-done(((bf16[768,768]{1,0:T(8,128)(2,1)}), bf16[192,768]{1,0:T(8,128)(2,1)}) %reduce-scatter.30.cloned.1.call-update) | async-done | bytes 294928 | tf_op jit(solution)/shard_map/reduce_scatter | solution.py:365
  534.7 36.2 %reduce-scatter.38.cloned.1.call-done = bf16[192,1536]{1,0:T(8,128)(2,1)} async-done(((bf16[768,1536]{1,0:T(8,128)(2,1)}), bf16[192,1536]{1,0:T(8,128)(2,1)}) %reduce-scatter.38.cloned.1.call-update) | async-done | bytes 589840 | tf_op jit(solution)/shard_map/reduce_scatter | solution.py:389
  570.9 43.1 %reduce-scatter.28.cloned.1.call-done = bf16[192,2304]{1,0:T(8,128)(2,1)} async-done(((bf16[768,2304]{1,0:T(8,128)(2,1)}), bf16[192,2304]{1,0:T(8,128)(2,1)}) %reduce-scatter.28.cloned.1.call-update) | async-done | bytes 884752 | tf_op jit(solution)/shard_map/reduce_scatter | solution.py:362
  614.0 50.4 %reduce-scatter.42.cloned.1.call-done = bf16[192,3072]{1,0:T(8,128)(2,1)} async-done(((bf16[768,3072]{1,0:T(8,128)(2,1)}), bf16[192,3072]{1,0:T(8,128)(2,1)}) %reduce-scatter.42.cloned.1.call-update) | async-done | bytes 1179664 | tf_op jit(solution)/shard_map/reduce_scatter | solution.py:395
  664.4 50.4 %reduce-scatter.44.cloned.1.call-done = bf16[768,768]{1,0:T(8,128)(2,1)} async-done(((bf16[3072,768]{1,0:T(8,128)(2,1)}), bf16[768,768]{1,0:T(8,128)(2,1)}) %reduce-scatter.44.cloned.1.call-update) | async-done | bytes 1179664 | tf_op jit(solution)/shard_map/reduce_scatter | solution.py:398
  714.8 50.5 %reduce-scatter.34.cloned.1.call-done = bf16[768,768]{1,0:T(8,128)(2,1)} async-done(((bf16[3072,768]{1,0:T(8,128)(2,1)}), bf16[768,768]{1,0:T(8,128)(2,1)}) %reduce-scatter.34.cloned.1.call-update) | async-done | bytes 1179664 | tf_op jit(solution)/shard_map/reduce_scatter | solution.py:371
  765.3 50.3 %reduce-scatter.32.cloned.1.call-done = bf16[192,3072]{1,0:T(8,128)(2,1)} async-done(((bf16[768,3072]{1,0:T(8,128)(2,1)}), bf16[192,3072]{1,0:T(8,128)(2,1)}) %reduce-scatter.32.cloned.1.call-update) | async-done | bytes 1179664 | tf_op jit(solution)/shard_map/reduce_scatter | solution.py:368
  815.6 547.2 %all-reduce.6 = (f32[2,192]{1,0:T(2,128)}, f32[6,192]{1,0:T(8,128)}, f32[768]{0:T(1024)}, f32[2,192]{1,0:T(2,128)}, f32[192,2304]{1,0:T(8,128)}, /*index=5*/f32[...) all-reduce(bf16[2,192]{1,0:T(2,128)(2,1)S(1)} %copy.241, ...), channel_id=1, replica_groups=mesh['batch'=8,'band'=4] {'batch'}, use_global_device_ids=true, to_apply=%region_29.30 | all-reduce | flops 3544704 | bytes 21271296 | tf_op jit(solution)/shard_map/psum | solution.py:420
  (494 shorter events, 337.3 us)
Async XLA Ops:
  20.5 15.9 %all-to-all-start = ((bf16[8,64,768]{2,1,0:T(8,128)(2,1)}), bf16[8,64,768]{2,1,0:T(8,128)(2,1)}, u32[]{:S(2)}, u32[]{:S(2)}) async-start(bf16[8,64,768]{2,1,0:T(8,128)(2,1)} %fusion.57), calls=%async_computation | async-start | bytes 1572864 | tf_op jit(solution)/shard_map/all_to_all | solution.py:169
  57.3 15.9 %all-to-all-start.2 = ((bf16[2,256,768]{2,0,1:T(2,128)(2,1)}), bf16[2,256,768]{2,0,1:T(2,128)(2,1)}, u32[]{:S(2)}, u32[]{:S(2)}) async-start(bf16[2,256,768]{2,0,1:T(2,128)(2,1)} %copy.182), calls=%async_computation.2 | async-start | bytes 1572864 | tf_op jit(solution)/shard_map/all_to_all | solution.py:187
  73.2 22.5 %all-to-all-start.4 = ((bf16[8,64,768]{2,1,0:T(8,128)(2,1)}), bf16[8,64,768]{2,1,0:T(8,128)(2,1)}, u32[]{:S(2)}, u32[]{:S(2)}) async-start(bf16[8,64,768]{2,1,0:T(8,128)(2,1)} %fusion.65), calls=%async_computation.4 | async-start | bytes 1572864 | tf_op jit(solution)/shard_map/all_to_all | solution.py:199
  95.7 15.9 %all-to-all-start.3 = ((bf16[8,64,768]{2,1,0:T(8,128)(2,1)}), bf16[8,64,768]{2,1,0:T(8,128)(2,1)}, u32[]{:S(2)}, u32[]{:S(2)}) async-start(bf16[8,64,768]{2,1,0:T(8,128)(2,1)} %add_convert_fusion.3), calls=%async_computation.3 | async-start | bytes 1572864 | tf_op jit(solution)/shard_map/all_to_all | solution.py:202
  131.4 16.1 %all-to-all-start.5 = ((bf16[2,256,768]{2,0,1:T(2,128)(2,1)}), bf16[2,256,768]{2,0,1:T(2,128)(2,1)}, u32[]{:S(2)}, u32[]{:S(2)}) async-start(bf16[2,256,768]{2,0,1:T(2,128)(2,1)} %copy.191), calls=%async_computation.5 | async-start | bytes 1572864 | tf_op jit(solution)/shard_map/all_to_all | solution.py:215
  175.7 16.3 %all-to-all-start.6 = ((bf16[8,64,768]{2,1,0:T(8,128)(2,1)}), bf16[8,64,768]{2,1,0:T(8,128)(2,1)}, u32[]{:S(2)}, u32[]{:S(2)}) async-start(bf16[8,64,768]{2,1,0:T(8,128)(2,1)} %multiply_convert_fusion.10), calls=%async_computation.6 | async-start | bytes 1572864 | tf_op jit(solution)/shard_map/all_to_all | solution.py:237
  245.2 26.7 %all-to-all-start.10 = ((bf16[2,256,768]{2,0,1:T(2,128)(2,1)}), bf16[2,256,768]{2,0,1:T(2,128)(2,1)}, u32[]{:S(2)}, u32[]{:S(2)}) async-start(bf16[2,256,768]{2,0,1:T(2,128)(2,1)} %copy.217), calls=%async_computation.10 | async-start | bytes 1572864 | tf_op jit(solution)/shard_map/all_to_all | solution.py:257
  271.9 15.9 %all-to-all-start.8 = ((bf16[8,64,768]{2,1,0:T(8,128)(2,1)}), bf16[8,64,768]{2,1,0:T(8,128)(2,1)}, u32[]{:S(2)}, u32[]{:S(2)}) async-start(bf16[8,64,768]{2,1,0:T(8,128)(2,1)} %multiply_convert_fusion.7), calls=%async_computation.8 | async-start | bytes 1572864 | tf_op jit(solution)/shard_map/all_to_all | solution.py:296
  276.2 148.3 %reduce-scatter.56.cloned.1.call-start = ((), (), s32[]{:S(2)}) async-start(), calls=%async_computation.40 | async-start | bytes 245760
  327.7 25.1 %all-to-all-start.9 = ((bf16[2,256,768]{2,0,1:T(2,128)(2,1)}), bf16[2,256,768]{2,0,1:T(2,128)(2,1)}, u32[]{:S(2)}, u32[]{:S(2)}) async-start(bf16[2,256,768]{2,0,1:T(2,128)(2,1)} %copy.211), calls=%async_computation.9 | async-start | bytes 1572864 | tf_op jit(solution)/shard_map/all_to_all | solution.py:315
  331.9 116.3 %reduce-scatter.50.cloned.1.call-start = ((), (), s32[]{:S(2)}) async-start(), calls=%async_computation.37 | async-start | bytes 245760
  337.4 112.4 %reduce-scatter.52.cloned.1.call-start = ((), (), s32[]{:S(2)}) async-start(), calls=%async_computation.38 | async-start | bytes 245760
  339.0 112.2 %reduce-scatter.54.cloned.1.call-start = ((), (), s32[]{:S(2)}) async-start(), calls=%async_computation.39 | async-start | bytes 245760
  352.7 105.3 %reduce-scatter.46.cloned.1.call-start = ((), (), s32[]{:S(2)}) async-start(), calls=%async_computation.35 | async-start | bytes 245760
  360.6 98.3 %reduce-scatter.48.cloned.1.call-start = ((), (), s32[]{:S(2)}) async-start(), calls=%async_computation.36 | async-start | bytes 245760
  373.2 104.2 %reduce-scatter.40.cloned.1.call-start = ((), (), s32[]{:S(2)}) async-start(), calls=%async_computation.32 | async-start | bytes 1474560 | tf_op jit(solution)/shard_map/reduce_scatter | solution.py:392
  376.4 129.4 %reduce-scatter.36.cloned.1.call-start = ((), (), s32[]{:S(2)}) async-start(), calls=%async_computation.30 | async-start | bytes 1474560 | tf_op jit(solution)/shard_map/reduce_scatter | solution.py:386
  379.8 155.0 %reduce-scatter.30.cloned.1.call-start = ((), (), s32[]{:S(2)}) async-start(), calls=%async_computation.27 | async-start | bytes 1474560 | tf_op jit(solution)/shard_map/reduce_scatter | solution.py:365
  383.0 187.9 %reduce-scatter.38.cloned.1.call-start = ((), (), s32[]{:S(2)}) async-start(), calls=%async_computation.31 | async-start | bytes 2949120 | tf_op jit(solution)/shard_map/reduce_scatter | solution.py:389
  387.5 226.5 %reduce-scatter.28.cloned.1.call-start = ((), (), s32[]{:S(2)}) async-start(), calls=%async_computation.26 | async-start | bytes 4423680 | tf_op jit(solution)/shard_map/reduce_scatter | solution.py:362
  393.3 271.1 %reduce-scatter.42.cloned.1.call-start = ((), (), s32[]{:S(2)}) async-start(), calls=%async_computation.33 | async-start | bytes 5898240 | tf_op jit(solution)/shard_map/reduce_scatter | solution.py:395
  400.7 314.1 %reduce-scatter.44.cloned.1.call-start = ((), (), s32[]{:S(2)}) async-start(), calls=%async_computation.34 | async-start | bytes 5898240 | tf_op jit(solution)/shard_map/reduce_scatter | solution.py:398
  408.0 357.3 %reduce-scatter.34.cloned.1.call-start = ((), (), s32[]{:S(2)}) async-start(), calls=%async_computation.29 | async-start | bytes 5898240 | tf_op jit(solution)/shard_map/reduce_scatter | solution.py:371
  415.1 400.5 %reduce-scatter.32.cloned.1.call-start = ((), (), s32[]{:S(2)}) async-start(), calls=%async_computation.28 | async-start | bytes 5898240 | tf_op jit(solution)/shard_map/reduce_scatter | solution.py:368
  (130 other events, 957.3 us)
Sparse Core Ops, SparseCore 0:
  280.1 21.9 reduce-scatter.55
  337.5 21.8 reduce-scatter.49
  361.9 19.7 reduce-scatter.51
  383.9 19.7 reduce-scatter.53
  406.6 19.7 reduce-scatter.45
  429.2 19.7 reduce-scatter.47
  451.6 25.7 reduce-scatter.39
  480.1 25.6 reduce-scatter.35
  509.0 25.7 reduce-scatter.29
  537.8 33.0 reduce-scatter.37
  573.5 40.4 reduce-scatter.27
  616.5 47.8 reduce-scatter.41
  667.0 47.8 reduce-scatter.43
  717.4 47.8 reduce-scatter.33
  767.7 47.8 reduce-scatter.31
where the time goes:
time: 1380 us; the launch traced here: 1370 us
  blocking collectives  560 us (41%)
  waiting for transfers between devices  403 us (29%)
  matrix products  156 us (11%)
  local copies, waits for them, and re-layouts  113 us (8%)
  other arithmetic  72 us (5%)
  starting transfers between devices  48.5 us (4%)
  between operations  16.2 us (1%)
    psum x1, blocking collectives, body(): lax.psum((enc_gains_grad, enc_shifts_grad, enc_wide_grad, enc_scales_grad...  547 us
    reduce_scatter x1, waiting for transfers between devices, body(): lax.psum_scatter(enc_reduce_grad.astype(jnp.bfloat16), 'band', scatter_di...  50.5 us
    reduce_scatter x1, waiting for transfers between devices, body(): lax.psum_scatter(reg_expand_grad.astype(jnp.bfloat16), 'band', scatter_di...  50.4 us
    reduce_scatter x1, waiting for transfers between devices, body(): lax.psum_scatter(reg_reduce_grad.astype(jnp.bfloat16), 'band', scatter_di...  50.4 us
    reduce_scatter x1, waiting for transfers between devices, body(): lax.psum_scatter(enc_expand_grad.astype(jnp.bfloat16), 'band', scatter_di...  50.3 us
    dot_general x9, matrix products, weight_grad(): jnp.einsum('nsi,nsj->ij', row_data, grad_rows, preferred_element_type=jnp...  48.5 us
    reduce_scatter x1, waiting for transfers between devices, body(): lax.psum_scatter(enc_project_grad.astype(jnp.bfloat16), 'band', scatter_d...  43.1 us
    reduce_scatter x1, waiting for transfers between devices, body(): lax.psum_scatter(reg_keyval_grad.astype(jnp.bfloat16), 'band', scatter_di...  36.2 us
  transfers between devices with their start and end apart: 26, of which 16 were waited for; matrix products, arithmetic and copies ran while one was open for 16% of the time, Pallas kernels for 0%

commit v1 on v0

v1 whole, which is shorter than its diff:
```python
import functools

import jax
import jax.numpy as jnp
from jax import lax
from jax.experimental import pallas as pl
from jax.experimental.pallas import tpu as pltpu
from jax.sharding import PartitionSpec as P

HEADS = 12
HD = 64
EPS = 1e-06
ROOT_HALF = 0.7071067811865476
INV_ROOT_TAU = 0.3989422804014327
NEG_LARGE = -1e30
F32 = jnp.float32
BF16 = jnp.bfloat16
VMEM_LIMIT = 56 * 1024 * 1024
LANES = 128


def dot(a, b):
    return lax.dot_general(a, b, (((1,), (0,)), ((), ())), preferred_element_type=F32)


def dot_nt(a, b):
    return lax.dot_general(a, b, (((1,), (1,)), ((), ())), preferred_element_type=F32)


def dot_tn(a, b):
    return lax.dot_general(a, b, (((0,), (0,)), ((), ())), preferred_element_type=F32)


def unit(values):
    row_mean = jnp.mean(values, -1, keepdims=True)
    centred = values - row_mean
    variance = jnp.mean(centred * centred, -1, keepdims=True)
    inv_std = lax.rsqrt(variance + EPS)
    return centred * inv_std, inv_std


def unit_back(grad_out, unit_rows, inv_std, gain):
    scaled = grad_out * gain
    first_term = jnp.mean(scaled, -1, keepdims=True)
    second_term = jnp.mean(scaled * unit_rows, -1, keepdims=True)
    return inv_std * (scaled - first_term - unit_rows * second_term)


def rows_sum(values):
    return jnp.sum(values, 0, keepdims=True)


def gate_and_slope(pre_act):
    bell = 0.5 * (1.0 + lax.erf(pre_act * ROOT_HALF))
    slope = bell + pre_act * INV_ROOT_TAU * jnp.exp(-0.5 * pre_act * pre_act)
    return (pre_act * bell).astype(BF16), slope.astype(BF16)


class Meta:
    def __init__(self, ref, images):
        self.ref, self.images = ref, images

    def bins(self):
        return self.ref[0]

    def band(self):
        return self.ref[1]

    def bin_of(self, image):
        return self.ref[2 + image]

    def keep_off(self, image):
        return self.ref[2 + self.images + image]

    def keep_count(self, image):
        return self.ref[2 + 2 * self.images + image]

    def pick_off(self, image):
        return self.ref[2 + 3 * self.images + image]

    def pick_count(self, image):
        return self.ref[2 + 4 * self.images + image]

    def segments(self, bin_now, kind, shape, dim, blank):
        rows = lax.broadcasted_iota(jnp.int32, shape, dim)
        owner = jnp.full(shape, blank, jnp.int32)
        for image in range(self.images):
            start = self.keep_off(image) if kind == "keep" else self.pick_off(image)
            count = self.keep_count(image) if kind == "keep" else self.pick_count(image)
            stop = start + jnp.where(self.bin_of(image) == bin_now, count, 0)
            owner = jnp.where((rows >= start) & (rows < stop), image, owner)
        return owner


def key_mask(meta, bin_now, query_kind, size):
    query_owner = meta.segments(bin_now, query_kind, (size, 1), 0, -2)
    key_owner = meta.segments(bin_now, "keep", (1, size), 1, -1)
    return query_owner == key_owner


def quarter_rows(meta, width, parts):
    part = width // parts
    row = lax.broadcasted_iota(jnp.int32, (part, width), 0) + meta.band() * part
    return (row == lax.broadcasted_iota(jnp.int32, (part, width), 1)).astype(BF16)


def lower_half():
    return lax.broadcasted_iota(jnp.int32, (1, LANES), 1) < HD


def attend_forward(query_of, key_of, value_of, mask_ref, store, size):
    low = lower_half()
    sides = (low.astype(BF16), (~low).astype(BF16))
    lane = lax.broadcasted_iota(jnp.int32, (size, LANES), 1)
    totals = jnp.zeros((size, LANES), F32)
    for pair in range(HEADS // 2):
        cols = slice(pair * LANES, (pair + 1) * LANES)
        query, key, value = query_of(cols), key_of(cols), value_of(cols)
        mixed = []
        for side in range(2):
            scores = dot_nt(query, key * sides[side]) * HD ** (-0.5)
            scores = jnp.where(mask_ref[...] > 0, scores, NEG_LARGE)
            row_top = jnp.max(scores, -1, keepdims=True)
            exp_scores = jnp.exp(scores - row_top)
            row_total = jnp.sum(exp_scores, -1, keepdims=True)
            weights = (exp_scores * (1.0 / row_total)).astype(BF16)
            totals = jnp.where(lane == 2 * pair + side, row_top + jnp.log(row_total), totals)
            mixed.append(dot(weights, value))
        store(cols, jnp.where(low, mixed[0], mixed[1]))
    return totals


def attend_backward(query_of, key_of, value_of, grad_of, totals, mask_ref, store):
    low = lower_half()
    sides = (low.astype(BF16), (~low).astype(BF16))
    for pair in range(HEADS // 2):
        cols = slice(pair * LANES, (pair + 1) * LANES)
        query, key, value, grad = query_of(cols), key_of(cols), value_of(cols), grad_of(cols)
        grad_query, grad_key, grad_value = [], [], []
        for side in range(2):
            head = 2 * pair + side
            scores = dot_nt(query, key * sides[side]) * HD ** (-0.5)
            scores = jnp.where(mask_ref[...] > 0, scores, NEG_LARGE)
            probs = jnp.exp(scores - totals[:, head : head + 1])
            grad_value.append(dot_tn(probs.astype(BF16), grad))
            grad_probs = dot_nt(grad, value * sides[side])
            inner = jnp.sum(grad_probs * probs, -1, keepdims=True)
            grad_scores = (probs * (grad_probs - inner)).astype(BF16)
            grad_query.append(dot(grad_scores, key))
            grad_key.append(dot_tn(grad_scores, query))
        store(
            cols,
            jnp.where(low, grad_query[0], grad_query[1]) * HD ** (-0.5),
            jnp.where(low, grad_key[0], grad_key[1]) * HD ** (-0.5),
            jnp.where(low, grad_value[0], grad_value[1]),
        )


def pack_rows(meta, bin_now, place_ref, sources, size):
    for _, packed in sources:
        packed[...] = jnp.zeros_like(packed)
    for image in range(meta.images):

        @pl.when(meta.bin_of(image) == bin_now)
        def _():
            row = lax.broadcasted_iota(jnp.int32, (size, size), 0)
            chosen = (row == place_ref[image : image + 1, :]).astype(BF16)
            for gathered, packed in sources:
                rows = jnp.concatenate(
                    [gathered[band, image] for band in range(gathered.shape[0])], 0
                )
                packed[...] += dot(chosen, rows)


class Weights:
    def __init__(self, sources, targets, sems):
        self.copies = [
            pltpu.make_async_copy(source, target, sems.at[i])
            for i, (source, target) in enumerate(zip(sources, targets, strict=True))
        ]

    def start(self):
        @pl.when(pl.program_id(0) == 0)
        def _():
            for copy in self.copies:
                copy.start()

    def wait(self, index):
        @pl.when(pl.program_id(0) == 0)
        def _():
            self.copies[index].wait()


def add_row(small_ref, row, values):
    small_ref[row : row + 1, :] += values


def first_step(refs):
    @pl.when(pl.program_id(0) == 0)
    def _():
        for ref in refs:
            ref[...] = jnp.zeros_like(ref)


def last_step(meta, write):
    @pl.when(pl.program_id(0) == meta.bins() - 1)
    def _():
        write()


def plan_kernel(images, counts_ref, band_ref, keep_ref, pick_ref, meta_ref, keep_place_ref, pick_place_ref, words):
    size = keep_ref.shape[1]
    before = (
        lax.broadcasted_iota(jnp.int32, (size, size), 0)
        <= lax.broadcasted_iota(jnp.int32, (size, size), 1)
    ).astype(BF16)
    keep, pick = keep_ref[...], pick_ref[...]
    keep_rank = dot(keep.astype(BF16), before).astype(jnp.int32) - 1
    pick_rank = dot(pick.astype(BF16), before).astype(jnp.int32) - 1
    for image in range(images):
        words[0, image] = jnp.sum(keep[image : image + 1, :]).astype(jnp.int32)
        words[1, image] = jnp.sum(pick[image : image + 1, :]).astype(jnp.int32)
        for row in (2, 3, 4):
            words[row, image] = 0

    def place(_, bins):
        def largest(image, best):
            open_now = words[4, image] == 0
            better = open_now & ((best < 0) | (counts_ref[image] > counts_ref[jnp.maximum(best, 0)]))
            return jnp.where(better, image, best)

        image = lax.fori_loop(0, images, largest, jnp.int32(-1))
        keep_count, pick_count = words[0, image], words[1, image]

        def first_fit(step, best):
            bin_now = images - 1 - step
            fits = (words[2, bin_now] + keep_count <= size) & (words[3, bin_now] + pick_count <= size)
            return jnp.where(fits, bin_now, best)

        bin_now = lax.fori_loop(0, images, first_fit, jnp.int32(0))
        meta_ref[2 + image] = bin_now
        meta_ref[2 + images + image] = words[2, bin_now]
        meta_ref[2 + 2 * images + image] = keep_count
        meta_ref[2 + 3 * images + image] = words[3, bin_now]
        meta_ref[2 + 4 * images + image] = pick_count
        words[2, bin_now] = words[2, bin_now] + keep_count
        words[3, bin_now] = words[3, bin_now] + pick_count
        words[4, image] = 1
        return jnp.maximum(bins, bin_now + 1)

    meta_ref[0] = lax.fori_loop(0, images, place, jnp.int32(0))
    meta_ref[1] = band_ref[0]
    for image in range(images):
        row = slice(image, image + 1)
        keep_place_ref[row, :] = jnp.where(
            keep[row, :] > 0, keep_rank[row, :] + meta_ref[2 + images + image], -1
        )
        pick_place_ref[row, :] = jnp.where(
            pick[row, :] > 0, pick_rank[row, :] + meta_ref[2 + 3 * images + image], -1
        )


def ffn_forward(normed, expand, wide_bias, reduce_weight, act_ref, slope_ref, width):
    total = None
    for start in range(0, expand.shape[1], width):
        cols = slice(start, start + width)
        act, slope = gate_and_slope(dot(normed, expand[:, cols]) + wide_bias[:, cols])
        act_ref[:, cols] = act
        slope_ref[:, cols] = slope
        part = dot(act, reduce_weight[cols, :])
        total = part if total is None else total + part
    return total


def ffn_backward(grad_low, slope_ref, normed_part, expand, reduce_weight, expand_acc, wide_ref, width):
    total = None
    for start in range(0, expand.shape[1], width):
        cols = slice(start, start + width)
        grad_act = dot_nt(grad_low, reduce_weight[cols, :])
        grad_pre = grad_act * slope_ref[:, cols].astype(F32)
        grad_pre_low = grad_pre.astype(BF16)
        wide_ref[0:1, cols] += rows_sum(grad_pre_low.astype(F32))
        expand_acc[:, cols] += dot(normed_part, grad_pre_low)
        part = dot_nt(grad_pre_low, expand[:, cols])
        total = part if total is None else total + part
    return total


def enc_forward_kernel(
    images,
    parts,
    meta_ref,
    place_ref,
    rows_ref,
    gains,
    shifts,
    wide_bias,
    scales,
    reg_gains,
    reg_shifts,
    project_hbm,
    output_hbm,
    expand_hbm,
    reduce_hbm,
    keyval_hbm,
    x_out,
    triple_out,
    totals_out,
    normed_t_out,
    mixed_t_out,
    branch_out,
    act_out,
    slope_out,
    middle_t_out,
    ffn_out,
    pair_t_out,
    pair_out,
    project,
    output,
    expand,
    reduce_weight,
    keyval,
    sems,
    packed,
    mask_ref,
    act_all,
    mixed_ref,
):
    meta = Meta(meta_ref, images)
    bin_now = pl.program_id(0)
    weights = Weights(
        (project_hbm, output_hbm, expand_hbm, reduce_hbm, keyval_hbm),
        (project, output, expand, reduce_weight, keyval),
        sems,
    )
    weights.start()
    size, width = packed.shape
    pack_rows(meta, bin_now, place_ref, ((rows_ref, packed),), size)
    mask_ref[...] = key_mask(meta, bin_now, "keep", size).astype(F32)
    part_of = quarter_rows(meta, width, parts)
    x = packed[...]
    x_out[...] = x.astype(BF16)
    unit_rows, _ = unit(x)
    normed = (unit_rows * gains[0:1, :] + shifts[0:1, :]).astype(BF16)
    normed_t_out[...] = dot_nt(part_of, normed).astype(BF16)
    weights.wait(0)
    triple_out[:, :width] = (dot(normed, project[:, :width]) + shifts[1:2, :]).astype(BF16)
    triple_out[:, width : 2 * width] = dot(normed, project[:, width : 2 * width]).astype(BF16)
    triple_out[:, 2 * width :] = (dot(normed, project[:, 2 * width :]) + shifts[2:3, :]).astype(BF16)

    def store(cols, mixed):
        mixed_ref[:, cols] = mixed.astype(BF16)

    totals_out[...] = attend_forward(
        lambda cols: triple_out[:, cols],
        lambda cols: triple_out[:, width + cols.start : width + cols.stop],
        lambda cols: triple_out[:, 2 * width + cols.start : 2 * width + cols.stop],
        mask_ref,
        store,
        size,
    )
    mixed = mixed_ref[...]
    mixed_t_out[...] = dot_nt(part_of, mixed).astype(BF16)
    weights.wait(1)
    branch = (dot(mixed, output[...]) + shifts[3:4, :]).astype(BF16)
    branch_out[...] = branch
    middle = x + scales[0:1, :] * branch.astype(F32)
    unit_rows, _ = unit(middle)
    normed = (unit_rows * gains[1:2, :] + shifts[4:5, :]).astype(BF16)
    middle_t_out[...] = dot_nt(part_of, normed).astype(BF16)
    weights.wait(2)
    weights.wait(3)
    part_width = expand.shape[1] // parts
    ffn = ffn_forward(normed, expand, wide_bias, reduce_weight, act_all, slope_out, part_width) + shifts[5:6, :]
    act_out[...] = act_all[:, pl.ds(pl.multiple_of(meta.band() * part_width, part_width), part_width)]
    ffn_out[...] = ffn
    encoded = middle + scales[1:2, :] * ffn
    unit_rows, _ = unit(encoded)
    pair_normed = (unit_rows * reg_gains[1:2, :] + reg_shifts[1:2, :]).astype(BF16)
    pair_t_out[...] = dot_nt(part_of, pair_normed).astype(BF16)
    weights.wait(4)
    pair_out[:, :width] = dot(pair_normed, keyval[:, :width]).astype(BF16)
    pair_out[:, width:] = (dot(pair_normed, keyval[:, width:]) + reg_shifts[3:4, :]).astype(BF16)


def reg_forward_kernel(
    images,
    parts,
    meta_ref,
    place_ref,
    rows_ref,
    grads_ref,
    pair_ref,
    gains,
    shifts,
    wide_bias,
    scales,
    query_hbm,
    output_hbm,
    expand_hbm,
    reduce_hbm,
    x_out,
    query_out,
    totals_out,
    normed_t_out,
    mixed_t_out,
    final_out,
    grad_mid_out,
    small_out,
    wide_out,
    grads_out,
    query_weight,
    output,
    expand,
    reduce_weight,
    sems,
    packed,
    packed_grad,
    mask_ref,
    act_all,
    slope_all,
    mixed_ref,
    expand_acc,
    reduce_acc,
):
    meta = Meta(meta_ref, images)
    bin_now = pl.program_id(0)
    weights = Weights(
        (query_hbm, output_hbm, expand_hbm, reduce_hbm),
        (query_weight, output, expand, reduce_weight),
        sems,
    )
    weights.start()
    first_step((small_out, wide_out, expand_acc, reduce_acc))
    size, width = packed.shape
    pack_rows(meta, bin_now, place_ref, ((rows_ref, packed), (grads_ref, packed_grad)), size)
    mask_ref[...] = key_mask(meta, bin_now, "pick", size).astype(F32)
    part_of = quarter_rows(meta, width, parts)
    z = packed[...]
    x_out[...] = z.astype(BF16)
    unit_rows, _ = unit(z)
    normed = (unit_rows * gains[0:1, :] + shifts[0:1, :]).astype(BF16)
    normed_t_out[...] = dot_nt(part_of, normed).astype(BF16)
    weights.wait(0)
    query_out[...] = (dot(normed, query_weight[...]) + shifts[2:3, :]).astype(BF16)

    def store(cols, mixed):
        mixed_ref[:, cols] = mixed.astype(BF16)

    totals_out[...] = attend_forward(
        lambda cols: query_out[:, cols],
        lambda cols: pair_ref[:, cols],
        lambda cols: pair_ref[:, width + cols.start : width + cols.stop],
        mask_ref,
        store,
        size,
    )
    mixed = mixed_ref[...]
    mixed_t_out[...] = dot_nt(part_of, mixed).astype(BF16)
    weights.wait(1)
    branch = (dot(mixed, output[...]) + shifts[4:5, :]).astype(BF16).astype(F32)
    middle = z + scales[0:1, :] * branch
    unit_rows, inv_std = unit(middle)
    normed = (unit_rows * gains[2:3, :] + shifts[5:6, :]).astype(BF16)
    normed_part = dot_nt(part_of, normed).astype(BF16)
    weights.wait(2)
    weights.wait(3)
    part_width = expand.shape[1] // parts
    ffn = ffn_forward(normed, expand, wide_bias, reduce_weight, act_all, slope_all, part_width) + shifts[6:7, :]
    final_out[...] = middle + scales[1:2, :] * ffn
    grad_final = packed_grad[...]
    add_row(small_out, 0, rows_sum(grad_final * ffn))
    grad_low = (scales[1:2, :] * grad_final).astype(BF16)
    add_row(small_out, 1, rows_sum(grad_low.astype(F32)))
    act_part = act_all[:, pl.ds(pl.multiple_of(meta.band() * part_width, part_width), part_width)]
    reduce_acc[...] += dot_tn(act_part, grad_low)
    grad_normed = ffn_backward(
        grad_low, slope_all, normed_part, expand, reduce_weight, expand_acc, wide_out, part_width
    )
    add_row(small_out, 2, rows_sum(grad_normed * unit_rows))
    add_row(small_out, 3, rows_sum(grad_normed))
    grad_mid = grad_final + unit_back(grad_normed, unit_rows, inv_std, gains[2:3, :])
    grad_mid_out[...] = grad_mid
    add_row(small_out, 4, rows_sum(grad_mid * branch))

    def write():
        rows = reduce_acc.shape[0]
        grads_out[:rows, :] = reduce_acc[...].astype(BF16)
        part = expand_acc.shape[0]
        for i in range(expand_acc.shape[1] // width):
            grads_out[rows + i * part : rows + (i + 1) * part, :] = expand_acc[
                :, i * width : (i + 1) * width
            ].astype(BF16)

    last_step(meta, write)


def reg_attention_kernel(
    images,
    parts,
    meta_ref,
    z_ref,
    query_ref,
    totals_ref,
    normed_t_ref,
    mixed_t_ref,
    grad_mid_ref,
    pair_ref,
    pair_t_ref,
    x_ref,
    enc_branch_ref,
    enc_ffn_ref,
    gains,
    scales,
    enc_scales,
    query_hbm,
    keyval_hbm,
    output_hbm,
    query_grad_out,
    encoded_grad_out,
    small_out,
    grads_out,
    query_weight,
    keyval,
    output,
    sems,
    mask_ref,
    mixed_grad_ref,
    query_back,
    pair_back,
    query_acc,
    pair_acc,
    output_acc,
):
    meta = Meta(meta_ref, images)
    bin_now = pl.program_id(0)
    weights = Weights((output_hbm, query_hbm, keyval_hbm), (output, query_weight, keyval), sems)
    weights.start()
    first_step((small_out, query_acc, pair_acc, output_acc))
    size, width = mixed_grad_ref.shape
    mask_ref[...] = key_mask(meta, bin_now, "pick", size).astype(F32)
    grad_mid = grad_mid_ref[...]
    branch_grad = (scales[0:1, :] * grad_mid).astype(BF16)
    output_acc[...] += dot(mixed_t_ref[...], branch_grad)
    add_row(small_out, 0, rows_sum(branch_grad.astype(F32)))
    weights.wait(0)
    mixed_grad_ref[...] = dot_nt(branch_grad, output[...]).astype(BF16)

    def store(cols, grad_query, grad_key, grad_value):
        query_back[:, cols] = grad_query.astype(BF16)
        pair_back[:, cols] = grad_key.astype(BF16)
        pair_back[:, width + cols.start : width + cols.stop] = grad_value.astype(BF16)

    attend_backward(
        lambda cols: query_ref[:, cols],
        lambda cols: pair_ref[:, cols],
        lambda cols: pair_ref[:, width + cols.start : width + cols.stop],
        lambda cols: mixed_grad_ref[:, cols],
        totals_ref[...],
        mask_ref,
        store,
    )
    grad_query, grad_pair = query_back[...], pair_back[...]
    query_acc[...] += dot(normed_t_ref[...], grad_query)
    pair_acc[...] += dot(pair_t_ref[...], grad_pair)
    add_row(small_out, 1, rows_sum(grad_query.astype(F32)))
    add_row(small_out, 2, rows_sum(grad_pair[:, width:].astype(F32)))
    weights.wait(1)
    query_side = dot_nt(grad_query, query_weight[...]).astype(BF16).astype(F32)
    weights.wait(2)
    pair_side = dot_nt(grad_pair, keyval[...]).astype(BF16).astype(F32)
    unit_rows, inv_std = unit(z_ref[...].astype(F32))
    add_row(small_out, 3, rows_sum(query_side * unit_rows))
    add_row(small_out, 4, rows_sum(query_side))
    query_grad_out[...] = grad_mid + unit_back(query_side, unit_rows, inv_std, gains[0:1, :])
    encoded = (
        x_ref[...].astype(F32)
        + enc_scales[0:1, :] * enc_branch_ref[...].astype(F32)
        + enc_scales[1:2, :] * enc_ffn_ref[...]
    )
    unit_rows, inv_std = unit(encoded)
    add_row(small_out, 5, rows_sum(pair_side * unit_rows))
    add_row(small_out, 6, rows_sum(pair_side))
    encoded_grad_out[...] = unit_back(pair_side, unit_rows, inv_std, gains[1:2, :])

    def write():
        part = query_acc.shape[0]
        grads_out[:part, :] = query_acc[...].astype(BF16)
        grads_out[part : 2 * part, :] = pair_acc[:, :width].astype(BF16)
        grads_out[2 * part : 3 * part, :] = pair_acc[:, width:].astype(BF16)
        grads_out[3 * part :, :] = output_acc[...].astype(BF16)

    last_step(meta, write)


def enc_ffn_kernel(
    images,
    parts,
    meta_ref,
    encoded_grad_ref,
    x_ref,
    branch_ref,
    ffn_ref,
    act_ref,
    slope_ref,
    middle_t_ref,
    gains,
    scales,
    expand_hbm,
    reduce_hbm,
    grad_mid_out,
    small_out,
    wide_out,
    grads_out,
    expand,
    reduce_weight,
    sems,
    expand_acc,
    reduce_acc,
):
    meta = Meta(meta_ref, images)
    weights = Weights((reduce_hbm, expand_hbm), (reduce_weight, expand), sems)
    weights.start()
    first_step((small_out, wide_out, expand_acc, reduce_acc))
    width = x_ref.shape[1]
    encoded_grad = encoded_grad_ref[...]
    add_row(small_out, 0, rows_sum(encoded_grad * ffn_ref[...]))
    grad_low = (scales[1:2, :] * encoded_grad).astype(BF16)
    add_row(small_out, 1, rows_sum(grad_low.astype(F32)))
    reduce_acc[...] += dot_tn(act_ref[...], grad_low)
    weights.wait(0)
    weights.wait(1)
    part_width = expand.shape[1] // parts
    grad_normed = ffn_backward(
        grad_low, slope_ref, middle_t_ref[...], expand, reduce_weight, expand_acc, wide_out, part_width
    )
    branch = branch_ref[...].astype(F32)
    unit_rows, inv_std = unit(x_ref[...].astype(F32) + scales[0:1, :] * branch)
    add_row(small_out, 2, rows_sum(grad_normed * unit_rows))
    add_row(small_out, 3, rows_sum(grad_normed))
    grad_mid = encoded_grad + unit_back(grad_normed, unit_rows, inv_std, gains[1:2, :])
    grad_mid_out[...] = grad_mid
    add_row(small_out, 4, rows_sum(grad_mid * branch))

    def write():
        rows = reduce_acc.shape[0]
        grads_out[:rows, :] = reduce_acc[...].astype(BF16)
        part = expand_acc.shape[0]
        for i in range(expand_acc.shape[1] // width):
            grads_out[rows + i * part : rows + (i + 1) * part, :] = expand_acc[
                :, i * width : (i + 1) * width
            ].astype(BF16)

    last_step(meta, write)


def enc_attention_kernel(
    images,
    parts,
    meta_ref,
    grad_mid_ref,
    x_ref,
    triple_ref,
    totals_ref,
    normed_t_ref,
    mixed_t_ref,
    gains,
    scales,
    output_hbm,
    project_hbm,
    patch_grad_out,
    small_out,
    grads_out,
    output,
    project,
    sems,
    mask_ref,
    mixed_grad_ref,
    triple_back,
    project_acc,
    output_acc,
):
    meta = Meta(meta_ref, images)
    bin_now = pl.program_id(0)
    weights = Weights((output_hbm, project_hbm), (output, project), sems)
    weights.start()
    first_step((small_out, project_acc, output_acc))
    size, width = mixed_grad_ref.shape
    mask_ref[...] = key_mask(meta, bin_now, "keep", size).astype(F32)
    grad_mid = grad_mid_ref[...]
    branch_grad = (scales[0:1, :] * grad_mid).astype(BF16)
    output_acc[...] += dot(mixed_t_ref[...], branch_grad)
    add_row(small_out, 0, rows_sum(branch_grad.astype(F32)))
    weights.wait(0)
    mixed_grad_ref[...] = dot_nt(branch_grad, output[...]).astype(BF16)

    def store(cols, grad_query, grad_key, grad_value):
        triple_back[:, cols] = grad_query.astype(BF16)
        triple_back[:, width + cols.start : width + cols.stop] = grad_key.astype(BF16)
        triple_back[:, 2 * width + cols.start : 2 * width + cols.stop] = grad_value.astype(BF16)

    attend_backward(
        lambda cols: triple_ref[:, cols],
        lambda cols: triple_ref[:, width + cols.start : width + cols.stop],
        lambda cols: triple_ref[:, 2 * width + cols.start : 2 * width + cols.stop],
        lambda cols: mixed_grad_ref[:, cols],
        totals_ref[...],
        mask_ref,
        store,
    )
    back = triple_back[...]
    project_acc[...] += dot(normed_t_ref[...], back)
    add_row(small_out, 1, rows_sum(back[:, :width].astype(F32)))
    add_row(small_out, 2, rows_sum(back[:, 2 * width :].astype(F32)))
    weights.wait(1)
    rows_grad = dot_nt(back, project[...]).astype(BF16).astype(F32)
    unit_rows, inv_std = unit(x_ref[...].astype(F32))
    add_row(small_out, 3, rows_sum(rows_grad * unit_rows))
    add_row(small_out, 4, rows_sum(rows_grad))
    patch_grad_out[...] = grad_mid + unit_back(rows_grad, unit_rows, inv_std, gains[0:1, :])

    def write():
        part = output_acc.shape[0]
        grads_out[:part, :] = output_acc[...].astype(BF16)
        for i in range(3):
            grads_out[(i + 1) * part : (i + 2) * part, :] = project_acc[
                :, i * width : (i + 1) * width
            ].astype(BF16)

    last_step(meta, write)


def unpack_kernel(meta_ref, keep_place, pick_place, final_ref, query_grad_ref, patch_grad_ref, final_out, query_grad_out, patch_grad_out):
    rows = keep_place.shape[0]
    size = final_ref.shape[0]
    lane = lax.broadcasted_iota(jnp.int32, (rows, size), 1)
    kept = (keep_place[...] == lane).astype(BF16)
    picked = (pick_place[...] == lane).astype(BF16)
    for chosen, source, target in (
        (picked, final_ref, final_out),
        (picked, query_grad_ref, query_grad_out),
        (kept, patch_grad_ref, patch_grad_out),
    ):
        values = source[...]
        high = values.astype(BF16)
        rest = (values - high.astype(F32)).astype(BF16)
        target[...] = dot(chosen, high) + dot(chosen, rest)


def whole(array):
    return pl.BlockSpec(array.shape, lambda *_: (0,) * array.ndim)


def by_bin(shape):
    return pl.BlockSpec((None,) + tuple(shape), lambda b, meta: (jnp.minimum(b, meta[0] - 1), 0, 0))


def for_used_bins(kernel):
    def guarded(meta_ref, *refs):
        @pl.when(pl.program_id(0) < meta_ref[0])
        def _():
            kernel(meta_ref, *refs)

    return guarded


IN_HBM = pl.BlockSpec(memory_space=pl.ANY)


def binned_call(kernel, name, images, meta, binned, full, hbm, binned_outs, full_outs, scratch, flops):
    operands = [meta] + [a for _, a in binned] + list(hbm)
    in_specs = [whole(a) if kind == "full" else by_bin(a.shape[1:]) for kind, a in binned]
    in_specs += [IN_HBM] * len(hbm)
    out_shape = [jax.ShapeDtypeStruct((images,) + s, t) for s, t in binned_outs]
    out_shape += [jax.ShapeDtypeStruct(s, t) for s, t in full_outs]
    out_specs = [by_bin(s) for s, _ in binned_outs]
    out_specs += [pl.BlockSpec(s, lambda *_: (0, 0)) for s, _ in full_outs]
    return pl.pallas_call(
        for_used_bins(kernel),
        name=name,
        out_shape=out_shape,
        grid_spec=pltpu.PrefetchScalarGridSpec(
            num_scalar_prefetch=1,
            grid=(images,),
            in_specs=in_specs,
            out_specs=out_specs,
            scratch_shapes=scratch,
        ),
        compiler_params=pltpu.CompilerParams(
            vmem_limit_bytes=VMEM_LIMIT, dimension_semantics=("arbitrary",)
        ),
        cost_estimate=pl.CostEstimate(flops=flops, bytes_accessed=20_000_000, transcendentals=0),
    )(*operands)


def body(
    batch_size,
    patches,
    queries,
    cotangent,
    counts,
    masked,
    enc_gains,
    enc_shifts,
    enc_widebias,
    enc_scales,
    enc_project,
    enc_output,
    enc_expand,
    enc_reduce,
    reg_gains,
    reg_shifts,
    reg_widebias,
    reg_scales,
    reg_query,
    reg_keyval,
    reg_output,
    reg_expand,
    reg_reduce,
):
    images, band_rows, width = patches.shape
    hidden = enc_expand.shape[1]
    band = lax.axis_index("band")
    masked_all = lax.all_gather(masked.astype(F32), "band", axis=1, tiled=True)
    size = masked_all.shape[1]
    parts = size // band_rows
    part, part_hidden = width // parts, hidden // parts
    patch_rows = lax.all_gather(patches, "band", axis=0)
    query_rows = lax.all_gather(queries, "band", axis=0)
    grad_rows = lax.all_gather(cotangent, "band", axis=0)

    real = lax.broadcasted_iota(jnp.int32, (images, size), 1) < counts[:, None]
    keep = jnp.where(real & (masked_all == 0), 1.0, 0.0).astype(F32)
    pick = jnp.where(real & (masked_all == 1), 1.0, 0.0).astype(F32)
    in_smem = pl.BlockSpec(memory_space=pltpu.SMEM)
    in_vmem = pl.BlockSpec(memory_space=pltpu.VMEM)
    meta, keep_place, pick_place = pl.pallas_call(
        functools.partial(plan_kernel, images),
        name="plan",
        out_shape=[
            jax.ShapeDtypeStruct((2 + 5 * images,), jnp.int32),
            jax.ShapeDtypeStruct((images, size), jnp.int32),
            jax.ShapeDtypeStruct((images, size), jnp.int32),
        ],
        in_specs=[in_smem, in_smem, in_vmem, in_vmem],
        out_specs=[in_smem, in_vmem, in_vmem],
        scratch_shapes=[pltpu.SMEM((5, images), jnp.int32)],
    )(counts, band.astype(jnp.int32).reshape(1), keep, pick)

    def both(*arrays):
        return [("full", a) for a in arrays]

    def cut(*arrays):
        return [("bin", a) for a in arrays]

    def vm(shape, dtype=BF16):
        return pltpu.VMEM(shape, dtype)

    enc_wide = enc_widebias.reshape(1, hidden)
    reg_wide = reg_widebias.reshape(1, hidden)
    (
        x,
        triple,
        enc_totals,
        enc_normed_t,
        enc_mixed_t,
        enc_branch,
        enc_act,
        enc_slope,
        enc_middle_t,
        enc_ffn,
        pair_t,
        pair,
    ) = binned_call(
        functools.partial(enc_forward_kernel, images, parts),
        "enc_forward",
        images,
        meta,
        both(keep_place, patch_rows, enc_gains, enc_shifts, enc_wide, enc_scales, reg_gains, reg_shifts),
        None,
        (enc_project, enc_output, enc_expand, enc_reduce, reg_keyval),
        [
            ((size, width), BF16),
            ((size, 3 * width), BF16),
            ((size, LANES), F32),
            ((part, size), BF16),
            ((part, size), BF16),
            ((size, width), BF16),
            ((size, part_hidden), BF16),
            ((size, hidden), BF16),
            ((part, size), BF16),
            ((size, width), F32),
            ((part, size), BF16),
            ((size, 2 * width), BF16),
        ],
        [],
        [
            vm(enc_project.shape),
            vm(enc_output.shape),
            vm(enc_expand.shape),
            vm(enc_reduce.shape),
            vm(reg_keyval.shape),
            pltpu.SemaphoreType.DMA((5,)),
            vm((size, width), F32),
            vm((size, size), F32),
            vm((size, hidden)),
            vm((size, width)),
        ],
        8_000_000_000,
    )
    small_rows = 8
    (
        z,
        reg_query_low,
        reg_totals,
        reg_normed_t,
        reg_mixed_t,
        final_rows,
        reg_grad_mid,
        reg_small,
        reg_wide_sum,
        reg_ffn_grads,
    ) = binned_call(
        functools.partial(reg_forward_kernel, images, parts),
        "reg_forward",
        images,
        meta,
        both(pick_place, query_rows, grad_rows)
        + cut(pair)
        + both(reg_gains, reg_shifts, reg_wide, reg_scales),
        None,
        (reg_query, reg_output, reg_expand, reg_reduce),
        [
            ((size, width), BF16),
            ((size, width), BF16),
            ((size, LANES), F32),
            ((part, size), BF16),
            ((part, size), BF16),
            ((size, width), F32),
            ((size, width), F32),
        ],
        [
            ((small_rows, width), F32),
            ((small_rows, hidden), F32),
            ((part_hidden + hidden // width * part, width), BF16),
        ],
        [
            vm(reg_query.shape),
            vm(reg_output.shape),
            vm(reg_expand.shape),
            vm(reg_reduce.shape),
            pltpu.SemaphoreType.DMA((4,)),
            vm((size, width), F32),
            vm((size, width), F32),
            vm((size, size), F32),
            vm((size, hidden)),
            vm((size, hidden)),
            vm((size, width)),
            vm((part, hidden), F32),
            vm((part_hidden, width), F32),
        ],
        8_000_000_000,
    )
    query_grad, encoded_grad, reg_attn_small, reg_attn_grads = binned_call(
        functools.partial(reg_attention_kernel, images, parts),
        "reg_attention_grad",
        images,
        meta,
        cut(z, reg_query_low, reg_totals, reg_normed_t, reg_mixed_t, reg_grad_mid, pair, pair_t, x, enc_branch, enc_ffn)
        + both(reg_gains, reg_scales, enc_scales),
        None,
        (reg_query, reg_keyval, reg_output),
        [((size, width), F32), ((size, width), F32)],
        [((small_rows, width), F32), ((4 * part, width), BF16)],
        [
            vm(reg_query.shape),
            vm(reg_keyval.shape),
            vm(reg_output.shape),
            pltpu.SemaphoreType.DMA((3,)),
            vm((size, size), F32),
            vm((size, width)),
            vm((size, width)),
            vm((size, 2 * width)),
            vm((part, width), F32),
            vm((part, 2 * width), F32),
            vm((part, width), F32),
        ],
        6_000_000_000,
    )
    enc_grad_mid, enc_small, enc_wide_sum, enc_ffn_grads = binned_call(
        functools.partial(enc_ffn_kernel, images, parts),
        "enc_ffn_grad",
        images,
        meta,
        cut(encoded_grad, x, enc_branch, enc_ffn, enc_act, enc_slope, enc_middle_t)
        + both(enc_gains, enc_scales),
        None,
        (enc_expand, enc_reduce),
        [((size, width), F32)],
        [
            ((small_rows, width), F32),
            ((small_rows, hidden), F32),
            ((part_hidden + hidden // width * part, width), BF16),
        ],
        [
            vm(enc_expand.shape),
            vm(enc_reduce.shape),
            pltpu.SemaphoreType.DMA((2,)),
            vm((part, hidden), F32),
            vm((part_hidden, width), F32),
        ],
        6_000_000_000,
    )
    patch_grad, enc_attn_small, enc_attn_grads = binned_call(
        functools.partial(enc_attention_kernel, images, parts),
        "enc_attention_grad",
        images,
        meta,
        cut(enc_grad_mid, x, triple, enc_totals, enc_normed_t, enc_mixed_t) + both(enc_gains, enc_scales),
        None,
        (enc_output, enc_project),
        [((size, width), F32)],
        [((small_rows, width), F32), ((4 * part, width), BF16)],
        [
            vm(enc_output.shape),
            vm(enc_project.shape),
            pltpu.SemaphoreType.DMA((2,)),
            vm((size, size), F32),
            vm((size, width)),
            vm((size, 3 * width)),
            vm((part, 3 * width), F32),
            vm((part, width), F32),
        ],
        6_000_000_000,
    )

    def own_places(places):
        mine = lax.dynamic_slice_in_dim(places, band * band_rows, band_rows, 1)
        return mine[:, :, None]

    by_image = pl.BlockSpec((None, band_rows, 1), lambda i, m: (i, 0, 0))
    bin_of_image = pl.BlockSpec((None, size, width), lambda i, m: (m[2 + i], 0, 0))
    image_out = pl.BlockSpec((None, band_rows, width), lambda i, m: (i, 0, 0))
    prediction, query_grad, patch_grad = pl.pallas_call(
        unpack_kernel,
        name="unpack",
        out_shape=[jax.ShapeDtypeStruct(patches.shape, F32)] * 3,
        grid_spec=pltpu.PrefetchScalarGridSpec(
            num_scalar_prefetch=1,
            grid=(images,),
            in_specs=[by_image, by_image, bin_of_image, bin_of_image, bin_of_image],
            out_specs=[image_out] * 3,
        ),
        compiler_params=pltpu.CompilerParams(vmem_limit_bytes=VMEM_LIMIT),
        cost_estimate=pl.CostEstimate(flops=2_000_000_000, bytes_accessed=20_000_000, transcendentals=0),
    )(meta, own_places(keep_place), own_places(pick_place), final_rows, query_grad, patch_grad)

    def reduce_batch(grads):
        return lax.psum(grads, "batch").astype(F32)

    def side_by_side(rows, pieces):
        return jnp.concatenate(jnp.split(rows, pieces, 0), 1)

    wide_pieces = hidden // width
    reg_ffn_grads = reduce_batch(reg_ffn_grads)
    reg_attn_grads = reduce_batch(reg_attn_grads)
    enc_ffn_grads = reduce_batch(enc_ffn_grads)
    enc_attn_grads = reduce_batch(enc_attn_grads)
    reg_reduce_grad = reg_ffn_grads[:part_hidden]
    reg_expand_grad = side_by_side(reg_ffn_grads[part_hidden:], wide_pieces)
    reg_query_grad = reg_attn_grads[:part]
    reg_keyval_grad = side_by_side(reg_attn_grads[part : 3 * part], 2)
    reg_output_grad = reg_attn_grads[3 * part :]
    enc_reduce_grad = enc_ffn_grads[:part_hidden]
    enc_expand_grad = side_by_side(enc_ffn_grads[part_hidden:], wide_pieces)
    enc_output_grad = enc_attn_grads[:part]
    enc_project_grad = side_by_side(enc_attn_grads[part:], 3)

    small = jnp.concatenate([reg_small, reg_attn_small, enc_small, enc_attn_small], 0)
    small = lax.dynamic_slice_in_dim(small, band * part, part, 1)
    wide = jnp.concatenate([reg_wide_sum[:1], enc_wide_sum[:1]], 0)
    wide = lax.dynamic_slice_in_dim(wide, band * part_hidden, part_hidden, 1)
    small, wide = lax.psum((small, wide), "batch")
    reg_s, reg_a, enc_s, enc_a = jnp.split(small, 4, 0)
    enc_gains_grad = jnp.stack([enc_a[3], enc_s[2]])
    enc_shifts_grad = jnp.stack([enc_a[4], enc_a[1], enc_a[2], enc_a[0], enc_s[3], enc_s[1]])
    enc_scales_grad = jnp.stack([enc_s[4], enc_s[0]])
    reg_gains_grad = jnp.stack([reg_a[3], reg_a[5], reg_s[2]])
    reg_shifts_grad = jnp.stack(
        [reg_a[4], reg_a[6], reg_a[1], reg_a[2], reg_a[0], reg_s[3], reg_s[1]]
    )
    reg_scales_grad = jnp.stack([reg_s[4], reg_s[0]])
    return (
        prediction,
        patch_grad,
        query_grad,
        enc_gains_grad,
        enc_shifts_grad,
        wide[1],
        enc_scales_grad,
        enc_project_grad,
        enc_output_grad,
        enc_expand_grad,
        enc_reduce_grad,
        reg_gains_grad,
        reg_shifts_grad,
        wide[0],
        reg_scales_grad,
        reg_query_grad,
        reg_keyval_grad,
        reg_output_grad,
        reg_expand_grad,
        reg_reduce_grad,
    )


def solution(mesh):
    token = P("batch", "band", None)
    in_specs = (token, token, token, P("batch"), P("batch", "band")) + (P(),) * 17
    by_row, by_col = P("band", None), P(None, "band")
    out_specs = (
        token,
        token,
        token,
        by_col,
        by_col,
        P("band"),
        by_col,
        by_row,
        by_row,
        by_row,
        by_row,
        by_col,
        by_col,
        P("band"),
        by_col,
        by_row,
        by_row,
        by_row,
        by_row,
        by_row,
    )
    return jax.shard_map(
        functools.partial(body, mesh.shape["batch"]),
        mesh=mesh,
        in_specs=in_specs,
        out_specs=out_specs,
        check_vma=False,
    )
```

time: 1380 us -> 468 us (0.34)
  blocking collectives: 560 us -> 78.8 us
  matrix products: 156 us -> 0 us
  waiting for transfers between devices: 403 us -> 247 us
  local copies, waits for them, and re-layouts: 113 us -> 13.7 us
  Pallas kernels: 0 us -> 97.3 us
  other arithmetic: 72 us -> 8.44 us
  starting transfers between devices: 48.5 us -> 0.15 us
    psum x1, blocking collectives: 547 us -> 72.7 us  [body(): small, wide = lax.psum((small, wide), 'batch')]
    reduce_scatter x9 -> x0, waiting for transfers between devices: 356 us -> none  [the longest x1 50.5 us: body(): lax.psum_scatter(enc_reduce_grad.astype(jnp.bfloat16), 'band', scatter_di...]
    psum x0 -> x1, waiting for transfers between devices: none -> 182 us  [reduce_batch(): return lax.psum(grads, 'batch').astype(F32)]
    dot_general x39 -> x0, matrix products: 156 us -> none  [the longest x9 48.5 us: weight_grad(): jnp.einsum('nsi,nsj->ij', row_data, grad_rows, preferred_element_type=jnp...]
    pallas_call x0 -> x7, Pallas kernels: none -> 97.3 us  [the longest x5 85.5 us: binned_call(): pl.pallas_call(for_used_bins(kernel), name=name, out_shape=out_shape, gri...]
    all_gather x0 -> x3, waiting for transfers between devices: none -> 62.6 us  [the longest x1 30.1 us: body(): grad_rows = lax.all_gather(cotangent, 'band', axis=0)]
    all_to_all x11 -> x0, waiting for transfers between devices: 47.5 us -> none  [the longest x1 10.3 us: body(): lax.all_to_all(reg_branch, 'band', split_axis=1, concat_axis=0, tiled=True)]
    all_to_all x11 -> x0, starting transfers between devices: 47.1 us -> none  [the longest x1 4.59 us: body(): lax.all_to_all((reg_grad_mid * reg_scales[0]).astype(jnp.bfloat16), 'band...]
  transfers between devices with their start and end apart: 26 -> 4, of which waited for: 16 -> 4; matrix products, arithmetic and copies ran while one was open for 16% -> 2% of each run, Pallas kernels for 0% -> 7%
where the time goes in v1:
time: 468 us; the launch traced here: 460 us
  waiting for transfers between devices  247 us (53%)
  Pallas kernels  97.3 us (21%)
  blocking collectives  78.8 us (17%)
  between operations  14.2 us (3%)
  local copies, waits for them, and re-layouts  13.7 us (3%)
  other arithmetic  8.44 us (2%)
    psum x1, waiting for transfers between devices, reduce_batch(): return lax.psum(grads, 'batch').astype(F32)  182 us
    pallas_call x5, Pallas kernels, binned_call(): pl.pallas_call(for_used_bins(kernel), name=name, out_shape=out_shape, gri...  85.5 us
    psum x1, blocking collectives, body(): small, wide = lax.psum((small, wide), 'batch')  72.7 us
    all_gather x1, waiting for transfers between devices, body(): grad_rows = lax.all_gather(cotangent, 'band', axis=0)  30.1 us
    all_gather x1, waiting for transfers between devices, body(): patch_rows = lax.all_gather(patches, 'band', axis=0)  21.1 us
    all_gather x1, waiting for transfers between devices, body(): query_rows = lax.all_gather(queries, 'band', axis=0)  11.4 us
  transfers between devices with their start and end apart: 4, of which 4 were waited for; matrix products, arithmetic and copies ran while one was open for 2% of the time, Pallas kernels for 7%

profile of v1, /device:TPU:0, one launch (start us, length us, event | category | flops | bytes accessed | tf_op | source)
XLA Modules:
  0.0 459.6 jit_solution(391569680758279654)
XLA Ops:
  9.5 6.2 %all-gather.3 = f32[4,64,8]{1,2,0:T(8,128)S(1)} all-gather(f32[1,64,8]{1,2,0:T(8,128)S(1)} %convert_bitcast_fusion), channel_id=1, replica_groups=mesh['batch'=8,'band'=4] {'band'}, dimensions={0}, use_global_device_ids=true | all-gather | bytes 10240 | tf_op jit(solution)/shard_map/all_gather | solution.py:824
  16.6 3.2 plan.1
  19.8 21.1 %all-gather.12.cloned.1.call-done = bf16[32,64,768]{2,1,0:T(8,128)(2,1)} async-done(((bf16[8,64,768]{2,1,0:T(8,128)(2,1)}), bf16[32,64,768]{2,1,0:T(8,128)(2,1)}) %all-gather.12.cloned.1.call-update) | async-done | bytes 3145744 | tf_op jit(solution)/shard_map/all_gather | solution.py:828
  40.9 18.7 %enc_forward.1 = (bf16[8,256,768]{2,1,0:T(8,128)(2,1)}, bf16[8,256,2304]{2,1,0:T(8,128)(2,1)}, f32[8,256,128]{2,1,0:T(8,128)}, bf16[8,192,256]{2,1,0:T(8,128)(2,...) custom-call(s32[42]{0:T(128)} %get-tuple-element.59.meta_ref, ...), custom_call_target="tpu_custom_call" | custom-call | flops 8000000000 | bytes 20000000 | tf_op jit(solution)/shard_map/enc_forward/pallas_call | solution.py:778
  59.6 11.4 %all-gather.8.cloned.1.call-done = bf16[32,64,768]{2,1,0:T(8,128)(2,1)} async-done(((bf16[8,64,768]{2,1,0:T(8,128)(2,1)}), bf16[32,64,768]{2,1,0:T(8,128)(2,1)}) %all-gather.8.cloned.1.call-update) | async-done | bytes 3145744 | tf_op jit(solution)/shard_map/all_gather | solution.py:829
  71.0 30.1 %all-gather.10.cloned.1.call-done = bf16[32,64,768]{2,1,0:T(8,128)(2,1)} async-done(((bf16[8,64,768]{2,1,0:T(8,128)(2,1)}), bf16[32,64,768]{2,1,0:T(8,128)(2,1)}) %all-gather.10.cloned.1.call-update) | async-done | bytes 3145744 | tf_op jit(solution)/shard_map/all_gather | solution.py:830
  101.1 23.3 %reg_forward.1 = (bf16[8,256,768]{2,1,0:T(8,128)(2,1)}, bf16[8,256,768]{2,1,0:T(8,128)(2,1)}, f32[8,256,128]{2,1,0:T(8,128)}, bf16[8,192,256]{2,1,0:T(8,128)(2,1...) custom-call(s32[42]{0:T(128)} %get-tuple-element.59.meta_ref, ...), custom_call_target="tpu_custom_call" | custom-call | flops 8000000000 | bytes 20000000 | tf_op jit(solution)/shard_map/reg_forward/pallas_call | solution.py:778
  124.5 15.8 %reg_attention_grad.1 = (f32[8,256,768]{2,1,0:T(8,128)}, f32[8,256,768]{2,1,0:T(8,128)}, f32[8,768]{1,0:T(8,128)}, bf16[768,768]{1,0:T(8,128)(2,1)}) custom-call(s32[42]{0:T(128)} %get-tuple-element.59.meta_ref, bf16[8,256,768]{2,1,0:T(8,128)(2,1)} %get-tuple-element.64.refs_0_, bf16[8,256,768]{2,1,0:T(8,128)(2,1)} %get-tuple-element.65.refs_1_, ...), custom_call_target="tpu_custom_call" | custom-call | flops 6000000000 | bytes 20000000 | tf_op jit(solution)/shard_map/reg_attention_grad/pallas_call | solution.py:778
  140.3 13.7 %enc_ffn_grad.1 = (f32[8,256,768]{2,1,0:T(8,128)}, f32[8,768]{1,0:T(8,128)}, f32[8,3072]{1,0:T(8,128)}, bf16[1536,768]{1,0:T(8,128)(2,1)}) custom-call(s32[42]{0:T(128)} %get-tuple-element.59.meta_ref, f32[8,256,768]{2,1,0:T(8,128)} %get-tuple-element.75.refs_0_, bf16[8,256,768]{2,1,0:T(8,128)(2,1)} %get-tuple-element.71.refs_8_.refs_1_, ...), custom_call_target="tpu_custom_call" | custom-call | flops 6000000000 | bytes 20000000 | tf_op jit(solution)/shard_map/enc_ffn_grad/pallas_call | solution.py:778
  154.0 13.9 %enc_attention_grad.1 = (f32[8,256,768]{2,1,0:T(8,128)}, f32[8,768]{1,0:T(8,128)}, bf16[768,768]{1,0:T(8,128)(2,1)}) custom-call(s32[42]{0:T(128)} %get-tuple-element.59.meta_ref, f32[8,256,768]{2,1,0:T(8,128)} %get-tuple-element.79.refs_0_, bf16[8,256,768]{2,1,0:T(8,128)(2,1)} %get-tuple-element.71.refs_8_.refs_1_, ...), custom_call_target="tpu_custom_call" | custom-call | flops 6000000000 | bytes 20000000 | tf_op jit(solution)/shard_map/enc_attention_grad/pallas_call | solution.py:778
  168.7 0.9 copy.50.keep_place
  169.6 0.9 copy.51.pick_place
  170.5 0.9 slice.138
  171.4 0.9 slice.137
  172.5 72.7 %all-reduce = (f32[32,192]{1,0:T(8,128)S(1)}, f32[2,768]{1,0:T(2,128)S(1)}) all-reduce(f32[32,192]{1,0:T(8,128)S(1)} %fusion.2, f32[2,768]{1,0:T(2,128)S(1)} %fusion.7), channel_id=1, replica_groups=mesh['batch'=8,'band'=4] {'batch'}, use_global_device_ids=true, to_apply=%region_0.1 | all-reduce | flops 7680 | bytes 61440 | tf_op jit(solution)/shard_map/psum | solution.py:1083
  248.8 8.6 %unpack.1 = (f32[8,64,768]{2,1,0:T(8,128)}, f32[8,64,768]{2,1,0:T(8,128)}, f32[8,64,768]{2,1,0:T(8,128)}) custom-call(s32[42]{0:T(128)} %get-tuple-element.59.meta_ref, s32[8,64,1]{2,1,0:T(8,128)} %copy.50.keep_place, s32[8,64,1]{2,1,0:T(8,128)} %copy.51.pick_place, f32[8,256,768]{2,1,0:T(8,128)} %get-tuple-element.63.final_ref, ...), custom_call_target="tpu_custom_call" | custom-call | flops 2000000000 | bytes 20000000 | tf_op jit(solution)/shard_map/unpack/pallas_call | solution.py:1044
  257.4 182.2 %all-reduce.4.cloned.1.call-done = (bf16[768,768]{1,0:T(8,128)(2,1)}, bf16[1536,768]{1,0:T(8,128)(2,1)}, bf16[768,768]{1,0:T(8,128)(2,1)}, bf16[1536,768]{1,0:T(8,128)(2,1)}) async-done(((bf16[768,768]{1,0:T(8,128)(2,1)}, bf16[1536,768]{1,0:T(8,128)(2,1)}, bf16[768,768]{1,0:T(8,128)(2,1)}, bf16[1536,768]{1,0:T(8,128)(2,1)}), (bf16[768,768]{1,0:T(8,128)(2,1)}, bf16[1536,768]{1,0:T(8,128)(2,1)}, ...) | async-done | bytes 7077904 | tf_op jit(solution)/shard_map/psum | solution.py:1059
  439.6 3.0 slice.170
  443.2 1.6 slice.185
  445.6 1.4 fusion.10
  447.0 1.1 pad_maximum_fusion.3
  448.1 1.3 pad_maximum_fusion.2
  449.5 1.7 pad_maximum_fusion.1
  451.1 1.7 pad_maximum_fusion
  (51 shorter events, 9.1 us)
Async XLA Ops:
  7.2 2.3 copy-start.8
  7.2 8.7 %copy-start.11 = (s32[8]{0:T(128)S(1)}, s32[8]{0:T(128)}, u32[]{:S(2)}) copy-start(s32[8]{0:T(128)} %counts_ref.1) | copy-start | bytes 100
  7.2 33.7 %all-gather.12.cloned.1.call-start = ((), (), s32[]{:S(2)}) async-start(), calls=%async_computation.2 | async-start | bytes 3932160 | tf_op jit(solution)/shard_map/all_gather | solution.py:828
  7.9 63.0 %all-gather.8.cloned.1.call-start = ((), (), s32[]{:S(2)}) async-start(), calls=%async_computation | async-start | bytes 3932160 | tf_op jit(solution)/shard_map/all_gather | solution.py:829
  8.7 92.4 %all-gather.10.cloned.1.call-start = ((), (), s32[]{:S(2)}) async-start(), calls=%async_computation.1 | async-start | bytes 3932160 | tf_op jit(solution)/shard_map/all_gather | solution.py:830
  9.4 430.2 %all-reduce.4.cloned.1.call-start = ((), (), s32[]{:S(2)}) async-start(), calls=%async_computation.3 | async-start | bytes 14155776 | tf_op jit(solution)/shard_map/psum | solution.py:1059
  168.0 0.7 copy-start.9
  168.0 0.7 copy-start.10
  168.0 4.4 copy-start.4
  168.0 4.4 copy-start.5
  168.0 4.4 copy-start.6
  168.0 4.4 copy-start.7
  439.6 3.0 copy-start
  439.6 3.1 copy-start.1
  443.1 1.7 copy-start.2
  443.2 2.5 copy-start.3
Sparse Core Ops, SparseCore 0:
  9.6 31.2 all-gather.11
  42.4 28.5 all-gather.7
  72.6 28.5 all-gather.9
  168.2 271.3 all-reduce.3

commit v2 on v1

--- a/solution.py
+++ b/solution.py
@@ -16,7 +16,9 @@
 F32 = jnp.float32
 BF16 = jnp.bfloat16
 VMEM_LIMIT = 56 * 1024 * 1024
+STEP_LIMIT = 16 * 1024 * 1024
 LANES = 128
+HEAD = 3
 
 
 def dot(a, b):
@@ -66,20 +68,23 @@
     def band(self):
         return self.ref[1]
 
+    def side(self):
+        return self.ref[2]
+
     def bin_of(self, image):
-        return self.ref[2 + image]
+        return self.ref[HEAD + image]
 
     def keep_off(self, image):
-        return self.ref[2 + self.images + image]
+        return self.ref[HEAD + self.images + image]
 
     def keep_count(self, image):
-        return self.ref[2 + 2 * self.images + image]
+        return self.ref[HEAD + 2 * self.images + image]
 
     def pick_off(self, image):
-        return self.ref[2 + 3 * self.images + image]
+        return self.ref[HEAD + 3 * self.images + image]
 
     def pick_count(self, image):
-        return self.ref[2 + 4 * self.images + image]
+        return self.ref[HEAD + 4 * self.images + image]
 
     def segments(self, bin_now, kind, shape, dim, blank):
         rows = lax.broadcasted_iota(jnp.int32, shape, dim)
@@ -202,6 +207,25 @@
             ref[...] = jnp.zeros_like(ref)
 
 
+def write_halves(meta, keep_out, send_out, write_first, write_second):
+    @pl.when(meta.side() == 0)
+    def _():
+        write_first(keep_out)
+        write_second(send_out)
+
+    @pl.when(meta.side() == 1)
+    def _():
+        write_first(send_out)
+        write_second(keep_out)
+
+
+def write_blocks(target, acc, start, stop, width, at=0):
+    part = acc.shape[0]
+    for i in range(start, stop):
+        row = at + (i - start) * part
+        target[row : row + part, :] = acc[:, i * width : (i + 1) * width].astype(BF16)
+
+
 def last_step(meta, write):
     @pl.when(pl.program_id(0) == meta.bins() - 1)
     def _():
@@ -238,11 +262,11 @@
             return jnp.where(fits, bin_now, best)
 
         bin_now = lax.fori_loop(0, images, first_fit, jnp.int32(0))
-        meta_ref[2 + image] = bin_now
-        meta_ref[2 + images + image] = words[2, bin_now]
-        meta_ref[2 + 2 * images + image] = keep_count
-        meta_ref[2 + 3 * images + image] = words[3, bin_now]
-        meta_ref[2 + 4 * images + image] = pick_count
+        meta_ref[HEAD + image] = bin_now
+        meta_ref[HEAD + images + image] = words[2, bin_now]
+        meta_ref[HEAD + 2 * images + image] = keep_count
+        meta_ref[HEAD + 3 * images + image] = words[3, bin_now]
+        meta_ref[HEAD + 4 * images + image] = pick_count
         words[2, bin_now] = words[2, bin_now] + keep_count
         words[3, bin_now] = words[3, bin_now] + pick_count
         words[4, image] = 1
@@ -250,13 +274,14 @@
 
     meta_ref[0] = lax.fori_loop(0, images, place, jnp.int32(0))
     meta_ref[1] = band_ref[0]
+    meta_ref[2] = band_ref[1]
     for image in range(images):
         row = slice(image, image + 1)
         keep_place_ref[row, :] = jnp.where(
-            keep[row, :] > 0, keep_rank[row, :] + meta_ref[2 + images + image], -1
+            keep[row, :] > 0, keep_rank[row, :] + meta_ref[HEAD + images + image], -1
         )
         pick_place_ref[row, :] = jnp.where(
-            pick[row, :] > 0, pick_rank[row, :] + meta_ref[2 + 3 * images + image], -1
+            pick[row, :] > 0, pick_rank[row, :] + meta_ref[HEAD + 3 * images + image], -1
         )
 
 
@@ -408,7 +433,8 @@
     grad_mid_out,
     small_out,
     wide_out,
-    grads_out,
+    keep_out,
+    send_out,
     query_weight,
     output,
     expand,
@@ -483,16 +509,16 @@
     grad_mid_out[...] = grad_mid
     add_row(small_out, 4, rows_sum(grad_mid * branch))
 
-    def write():
-        rows = reduce_acc.shape[0]
-        grads_out[:rows, :] = reduce_acc[...].astype(BF16)
-        part = expand_acc.shape[0]
-        for i in range(expand_acc.shape[1] // width):
-            grads_out[rows + i * part : rows + (i + 1) * part, :] = expand_acc[
-                :, i * width : (i + 1) * width
-            ].astype(BF16)
-
-    last_step(meta, write)
+    last_step(
+        meta,
+        lambda: write_halves(
+            meta,
+            keep_out,
+            send_out,
+            lambda out: write_blocks(out, reduce_acc, 0, 1, width),
+            lambda out: write_blocks(out, expand_acc, 0, parts, width),
+        ),
+    )
 
 
 def reg_attention_kernel(
@@ -519,7 +545,8 @@
     query_grad_out,
     encoded_grad_out,
     small_out,
-    grads_out,
+    keep_out,
+    send_out,
     query_weight,
     keyval,
     output,
@@ -583,14 +610,16 @@
     add_row(small_out, 6, rows_sum(pair_side))
     encoded_grad_out[...] = unit_back(pair_side, unit_rows, inv_std, gains[1:2, :])
 
-    def write():
-        part = query_acc.shape[0]
-        grads_out[:part, :] = query_acc[...].astype(BF16)
-        grads_out[part : 2 * part, :] = pair_acc[:, :width].astype(BF16)
-        grads_out[2 * part : 3 * part, :] = pair_acc[:, width:].astype(BF16)
-        grads_out[3 * part :, :] = output_acc[...].astype(BF16)
-
-    last_step(meta, write)
+    def write_first(out):
+        write_blocks(out, query_acc, 0, 1, width)
+        write_blocks(out, output_acc, 0, 1, width, query_acc.shape[0])
+
+    last_step(
+        meta,
+        lambda: write_halves(
+            meta, keep_out, send_out, write_first, lambda out: write_blocks(out, pair_acc, 0, 2, width)
+        ),
+    )
 
 
 def enc_ffn_kernel(
@@ -611,7 +640,8 @@
     grad_mid_out,
     small_out,
     wide_out,
-    grads_out,
+    keep_out,
+    send_out,
     expand,
     reduce_weight,
     sems,
@@ -642,16 +672,16 @@
     grad_mid_out[...] = grad_mid
     add_row(small_out, 4, rows_sum(grad_mid * branch))
 
-    def write():
-        rows = reduce_acc.shape[0]
-        grads_out[:rows, :] = reduce_acc[...].astype(BF16)
-        part = expand_acc.shape[0]
-        for i in range(expand_acc.shape[1] // width):
-            grads_out[rows + i * part : rows + (i + 1) * part, :] = expand_acc[
-                :, i * width : (i + 1) * width
-            ].astype(BF16)
-
-    last_step(meta, write)
+    last_step(
+        meta,
+        lambda: write_halves(
+            meta,
+            keep_out,
+            send_out,
+            lambda out: write_blocks(out, reduce_acc, 0, 1, width),
+            lambda out: write_blocks(out, expand_acc, 0, parts, width),
+        ),
+    )
 
 
 def enc_attention_kernel(
@@ -666,11 +696,17 @@
     mixed_t_ref,
     gains,
     scales,
+    reg_small,
+    reg_attn_small,
+    enc_small,
+    reg_wide,
+    enc_wide,
     output_hbm,
     project_hbm,
     patch_grad_out,
     small_out,
-    grads_out,
+    keep_out,
+    send_out,
     output,
     project,
     sems,
@@ -719,18 +755,30 @@
     add_row(small_out, 4, rows_sum(rows_grad))
     patch_grad_out[...] = grad_mid + unit_back(rows_grad, unit_rows, inv_std, gains[0:1, :])
 
-    def write():
+    def write_first(out):
         part = output_acc.shape[0]
-        grads_out[:part, :] = output_acc[...].astype(BF16)
-        for i in range(3):
-            grads_out[(i + 1) * part : (i + 2) * part, :] = project_acc[
-                :, i * width : (i + 1) * width
-            ].astype(BF16)
-
-    last_step(meta, write)
-
-
-def unpack_kernel(meta_ref, keep_place, pick_place, final_ref, query_grad_ref, patch_grad_ref, final_out, query_grad_out, patch_grad_out):
+        write_blocks(out, output_acc, 0, 1, width)
+        write_blocks(out, project_acc, 0, 1, width, part)
+        out[2 * part :, :] = jnp.zeros_like(out[2 * part :, :])
+        part_of = quarter_rows(meta, width, parts)
+        at = 2 * part
+        for small in (reg_small, reg_attn_small, enc_small, small_out):
+            rows = small.shape[0]
+            out[at : at + rows, :part] = dot_nt(small[...].astype(BF16), part_of).astype(BF16)
+            at += rows
+        mine = pl.ds(pl.multiple_of(meta.band() * width, width), width)
+        out[at : at + 8, :] = reg_wide[:, mine].astype(BF16)
+        out[at + 8 : at + 16, :] = enc_wide[:, mine].astype(BF16)
+
+    def write_second(out):
+        part = output_acc.shape[0]
+        write_blocks(out, project_acc, 1, 3, width)
+        out[2 * part :, :] = jnp.zeros_like(out[2 * part :, :])
+
+    last_step(meta, lambda: write_halves(meta, keep_out, send_out, write_first, write_second))
+
+
+def unpack_kernel(meta_ref, _, keep_place, pick_place, final_ref, query_grad_ref, patch_grad_ref, final_out, query_grad_out, patch_grad_out):
     rows = keep_place.shape[0]
     size = final_ref.shape[0]
     lane = lax.broadcasted_iota(jnp.int32, (rows, size), 1)
@@ -756,7 +804,7 @@
 
 
 def for_used_bins(kernel):
-    def guarded(meta_ref, *refs):
+    def guarded(meta_ref, _, *refs):
         @pl.when(pl.program_id(0) < meta_ref[0])
         def _():
             kernel(meta_ref, *refs)
@@ -765,17 +813,19 @@
 
 
 IN_HBM = pl.BlockSpec(memory_space=pl.ANY)
-
-
-def binned_call(kernel, name, images, meta, binned, full, hbm, binned_outs, full_outs, scratch, flops):
-    operands = [meta] + [a for _, a in binned] + list(hbm)
-    in_specs = [whole(a) if kind == "full" else by_bin(a.shape[1:]) for kind, a in binned]
+SHORT = pl.CostEstimate(flops=2_000_000_000, bytes_accessed=1_000_000, transcendentals=0)
+LONG = pl.CostEstimate(flops=20_000_000_000, bytes_accessed=10_000_000, transcendentals=0)
+
+
+def binned_call(kernel, name, images, chain, meta, binned, hbm, binned_outs, full_outs, scratch):
+    operands = [meta, chain.last] + [a for _, a in binned] + list(hbm)
+    in_specs = [IN_HBM] + [whole(a) if kind == "full" else by_bin(a.shape[1:]) for kind, a in binned]
     in_specs += [IN_HBM] * len(hbm)
     out_shape = [jax.ShapeDtypeStruct((images,) + s, t) for s, t in binned_outs]
     out_shape += [jax.ShapeDtypeStruct(s, t) for s, t in full_outs]
     out_specs = [by_bin(s) for s, _ in binned_outs]
     out_specs += [pl.BlockSpec(s, lambda *_: (0, 0)) for s, _ in full_outs]
-    return pl.pallas_call(
+    outs = pl.pallas_call(
         for_used_bins(kernel),
         name=name,
         out_shape=out_shape,
@@ -789,8 +839,174 @@
         compiler_params=pltpu.CompilerParams(
             vmem_limit_bytes=VMEM_LIMIT, dimension_semantics=("arbitrary",)
         ),
-        cost_estimate=pl.CostEstimate(flops=flops, bytes_accessed=20_000_000, transcendentals=0),
+        cost_estimate=LONG,
     )(*operands)
+    chain.last = outs[-1]
+    return outs
+
+
+def merge_kernel(bit, place, mine, got, own, send):
+    rows = own.shape[0]
+
+    def half(side):
+        at = pl.ds(pl.multiple_of(side * rows, rows), rows)
+        return (mine[at, :].astype(F32) + got[at, :].astype(F32)).astype(BF16)
+
+    own[...] = half(place[bit])
+    send[...] = half(1 - place[bit])
+
+
+def deal_kernel(place, mine, got, own, *sends):
+    rows = own.shape[0]
+    for offset, out in enumerate((own,) + sends):
+        at = pl.ds(pl.multiple_of((place[3] ^ offset) * rows, rows), rows)
+        out[...] = (mine[at, :].astype(F32) + got[at, :].astype(F32)).astype(BF16)
+
+
+def add_kernel(place, mine, *refs):
+    *parts, out = refs
+    total = mine[...].astype(F32)
+    for part in parts:
+        total += part[...].astype(F32)
+    out[...] = total.astype(BF16)
+
+
+def assemble_kernel(bit, place, mine, got, out):
+    rows = mine.shape[0]
+    out[pl.ds(pl.multiple_of(place[bit] * rows, rows), rows), :] = mine[...]
+    out[pl.ds(pl.multiple_of((1 - place[bit]) * rows, rows), rows), :] = got[...]
+
+
+def gather_kernel(place, *refs):
+    *pieces, out = refs
+    rows = pieces[0].shape[0]
+    for offset, piece in enumerate(pieces):
+        out[pl.ds(pl.multiple_of((place[3] ^ offset) * rows, rows), rows), :] = piece[...]
+
+
+def finish_kernel(layouts, place, half, got, *outs):
+    def write(halves):
+        targets = iter(outs)
+        for layout, source in zip(layouts, halves, strict=True):
+            for kind, start, count in layout:
+                out = next(targets)
+                if kind == "rows":
+                    out[...] = source[start : start + count, :].astype(F32)
+                else:
+                    rows, width = out.shape[0], source.shape[1]
+                    for i in range(count):
+                        out[:, i * width : (i + 1) * width] = source[
+                            start + i * rows : start + (i + 1) * rows, :
+                        ].astype(F32)
+
+    @pl.when(place[0] == 0)
+    def _():
+        write((half, got))
+
+    @pl.when(place[0] == 1)
+    def _():
+        write((got, half))
+
+
+class Chain:
+    def __init__(self, first):
+        self.last = first
+
+
+class Reduction:
+    def __init__(self, batch_size, chain, place, name, halves, layouts, outs):
+        self.batch_size, self.chain, self.place, self.name = batch_size, chain, place, name
+        self.layouts, self.outs = layouts, outs
+        self.mine, send = halves
+        self.line = batch_size // 2 == 4
+        self.got = self.exchange(send, 1)
+
+    def exchange(self, array, offset):
+        return lax.ppermute(array, "batch", [(i, i ^ offset) for i in range(self.batch_size)])
+
+    def call(self, kernel, step, out_shape, *arrays):
+        count = len(arrays)
+
+        def copied_in(place, _, *refs):
+            sources, outs = refs[:count], refs[count : -count - 1]
+            copies, sems = refs[-count - 1 : -1], refs[-1]
+            moves = [
+                pltpu.make_async_copy(source, copy, sems.at[i])
+                for i, (source, copy) in enumerate(zip(sources, copies, strict=True))
+            ]
+            for move in moves:
+                move.start()
+            for move in moves:
+                move.wait()
+            kernel(place, *copies, *outs)
+
+        in_vmem = pl.BlockSpec(memory_space=pltpu.VMEM)
+        out = pl.pallas_call(
+            copied_in,
+            name=self.name + "_" + step,
+            out_shape=out_shape,
+            in_specs=[pl.BlockSpec(memory_space=pltpu.SMEM)] + [IN_HBM] * (count + 1),
+            out_specs=jax.tree.map(lambda _: in_vmem, out_shape),
+            scratch_shapes=[pltpu.VMEM(a.shape, a.dtype) for a in arrays]
+            + [pltpu.SemaphoreType.DMA((count,))],
+            compiler_params=pltpu.CompilerParams(vmem_limit_bytes=STEP_LIMIT),
+            cost_estimate=SHORT,
+        )(self.place, self.chain.last, *arrays)
+        self.chain.last = out[0] if isinstance(out, (list, tuple)) else out
+        return out
+
+    def shape(self, numerator, denominator):
+        rows, width = self.mine.shape
+        return jax.ShapeDtypeStruct((rows * numerator // denominator, width), BF16)
+
+    def merge(self, bit):
+        if not self.line:
+            if bit == 1:
+                self.sum_line()
+            return
+        self.mine, send = self.call(
+            functools.partial(merge_kernel, bit), f"merge{bit}", [self.shape(1, 2)] * 2, self.mine, self.got
+        )
+        self.got = self.exchange(send, 1 << bit)
+
+    def add(self):
+        if self.line:
+            self.mine = self.call(add_kernel, "add", self.shape(1, 1), self.mine, self.got)
+            self.got = self.exchange(self.mine, 4)
+
+    def assemble(self, bit):
+        if self.line:
+            self.mine = self.call(
+                functools.partial(assemble_kernel, bit), f"assemble{bit}", self.shape(2, 1), self.mine, self.got
+            )
+        if self.line or bit == 1:
+            self.got = self.exchange(self.mine, 1 << (bit - 1))
+
+    def sum_line(self):
+        groups = [list(range(first, self.batch_size, 2)) for first in range(2)]
+        self.mine = lax.psum(self.mine + self.got, "batch", axis_index_groups=groups)
+
+    def deal(self):
+        if not self.line:
+            self.sum_line()
+            return
+        self.mine, *sends = self.call(deal_kernel, "deal", [self.shape(1, 4)] * 4, self.mine, self.got)
+        self.parts = [self.exchange(send, 2 * (i + 1)) for i, send in enumerate(sends)]
+
+    def total(self):
+        if self.line:
+            self.mine = self.call(add_kernel, "total", self.shape(1, 1), self.mine, *self.parts)
+            self.parts = [self.exchange(self.mine, 2 * (i + 1)) for i in range(3)]
+
+    def gather(self):
+        if self.line:
+            self.mine = self.call(gather_kernel, "gather", self.shape(4, 1), self.mine, *self.parts)
+        self.got = self.exchange(self.mine, 1)
+
+    def finish(self):
+        return self.call(
+            functools.partial(finish_kernel, self.layouts), "finish", list(self.outs), self.mine, self.got
+        )
 
 
 def body(
@@ -821,12 +1037,13 @@
     images, band_rows, width = patches.shape
     hidden = enc_expand.shape[1]
     band = lax.axis_index("band")
+    batch = lax.axis_index("batch")
+    side = lax.rem(batch, 2)
     masked_all = lax.all_gather(masked.astype(F32), "band", axis=1, tiled=True)
     size = masked_all.shape[1]
     parts = size // band_rows
     part, part_hidden = width // parts, hidden // parts
-    patch_rows = lax.all_gather(patches, "band", axis=0)
-    query_rows = lax.all_gather(queries, "band", axis=0)
+    token_rows = lax.all_gather(jnp.where(masked[:, :, None] == 0, patches, queries), "band", axis=0)
     grad_rows = lax.all_gather(cotangent, "band", axis=0)
 
     real = lax.broadcasted_iota(jnp.int32, (images, size), 1) < counts[:, None]
@@ -838,14 +1055,24 @@
         functools.partial(plan_kernel, images),
         name="plan",
         out_shape=[
-            jax.ShapeDtypeStruct((2 + 5 * images,), jnp.int32),
+            jax.ShapeDtypeStruct((HEAD + 5 * images,), jnp.int32),
             jax.ShapeDtypeStruct((images, size), jnp.int32),
             jax.ShapeDtypeStruct((images, size), jnp.int32),
         ],
         in_specs=[in_smem, in_smem, in_vmem, in_vmem],
         out_specs=[in_smem, in_vmem, in_vmem],
         scratch_shapes=[pltpu.SMEM((5, images), jnp.int32)],
-    )(counts, band.astype(jnp.int32).reshape(1), keep, pick)
+    )(counts, jnp.stack([band, side]), keep, pick)
+
+    chain = Chain(keep_place)
+    place = jnp.stack([side, lax.rem(batch // 2, 2), lax.rem(batch // 4, 2), batch // 2])
+    weight = functools.partial(jax.ShapeDtypeStruct, dtype=F32)
+
+    def reduction(name, halves, layouts, outs):
+        return Reduction(batch_size, chain, place, name, halves, layouts, outs)
+
+    ffn_layout = ([("rows", 0, part_hidden)], [("blocks", 0, parts)])
+    ffn_outs = (weight((part_hidden, width)), weight((part, hidden)))
 
     def both(*arrays):
         return [("full", a) for a in arrays]
@@ -875,9 +1102,9 @@
         functools.partial(enc_forward_kernel, images, parts),
         "enc_forward",
         images,
+        chain,
         meta,
-        both(keep_place, patch_rows, enc_gains, enc_shifts, enc_wide, enc_scales, reg_gains, reg_shifts),
-        None,
+        both(keep_place, token_rows, enc_gains, enc_shifts, enc_wide, enc_scales, reg_gains, reg_shifts),
         (enc_project, enc_output, enc_expand, enc_reduce, reg_keyval),
         [
             ((size, width), BF16),
@@ -906,9 +1133,8 @@
             vm((size, hidden)),
             vm((size, width)),
         ],
-        8_000_000_000,
-    )
-    small_rows = 8
+    )
+    small_rows, extra = 8, 64
     (
         z,
         reg_query_low,
@@ -919,16 +1145,16 @@
         reg_grad_mid,
         reg_small,
         reg_wide_sum,
-        reg_ffn_grads,
+        *reg_ffn_grads,
     ) = binned_call(
         functools.partial(reg_forward_kernel, images, parts),
         "reg_forward",
         images,
+        chain,
         meta,
-        both(pick_place, query_rows, grad_rows)
+        both(pick_place, token_rows, grad_rows)
         + cut(pair)
         + both(reg_gains, reg_shifts, reg_wide, reg_scales),
-        None,
         (reg_query, reg_output, reg_expand, reg_reduce),
         [
             ((size, width), BF16),
@@ -942,7 +1168,8 @@
         [
             ((small_rows, width), F32),
             ((small_rows, hidden), F32),
-            ((part_hidden + hidden // width * part, width), BF16),
+            ((part_hidden, width), BF16),
+            ((part_hidden, width), BF16),
         ],
         [
             vm(reg_query.shape),
@@ -959,19 +1186,19 @@
             vm((part, hidden), F32),
             vm((part_hidden, width), F32),
         ],
-        8_000_000_000,
-    )
-    query_grad, encoded_grad, reg_attn_small, reg_attn_grads = binned_call(
+    )
+    reg_ffn = reduction("reg_ffn", reg_ffn_grads, ffn_layout, ffn_outs)
+    query_grad, encoded_grad, reg_attn_small, *reg_attn_grads = binned_call(
         functools.partial(reg_attention_kernel, images, parts),
         "reg_attention_grad",
         images,
+        chain,
         meta,
         cut(z, reg_query_low, reg_totals, reg_normed_t, reg_mixed_t, reg_grad_mid, pair, pair_t, x, enc_branch, enc_ffn)
         + both(reg_gains, reg_scales, enc_scales),
-        None,
         (reg_query, reg_keyval, reg_output),
         [((size, width), F32), ((size, width), F32)],
-        [((small_rows, width), F32), ((4 * part, width), BF16)],
+        [((small_rows, width), F32)] + [((2 * part, width), BF16)] * 2,
         [
             vm(reg_query.shape),
             vm(reg_keyval.shape),
@@ -985,22 +1212,29 @@
             vm((part, 2 * width), F32),
             vm((part, width), F32),
         ],
-        6_000_000_000,
-    )
-    enc_grad_mid, enc_small, enc_wide_sum, enc_ffn_grads = binned_call(
+    )
+    reg_attn = reduction(
+        "reg_attention",
+        reg_attn_grads,
+        ([("rows", 0, part), ("rows", part, part)], [("blocks", 0, 2)]),
+        (weight((part, width)), weight((part, width)), weight((part, 2 * width))),
+    )
+    reg_ffn.deal()
+    enc_grad_mid, enc_small, enc_wide_sum, *enc_ffn_grads = binned_call(
         functools.partial(enc_ffn_kernel, images, parts),
         "enc_ffn_grad",
         images,
+        chain,
         meta,
         cut(encoded_grad, x, enc_branch, enc_ffn, enc_act, enc_slope, enc_middle_t)
         + both(enc_gains, enc_scales),
-        None,
         (enc_expand, enc_reduce),
         [((size, width), F32)],
         [
             ((small_rows, width), F32),
             ((small_rows, hidden), F32),
-            ((part_hidden + hidden // width * part, width), BF16),
+            ((part_hidden, width), BF16),
+            ((part_hidden, width), BF16),
         ],
         [
             vm(enc_expand.shape),
@@ -1009,18 +1243,21 @@
             vm((part, hidden), F32),
             vm((part_hidden, width), F32),
         ],
-        6_000_000_000,
-    )
-    patch_grad, enc_attn_small, enc_attn_grads = binned_call(
+    )
+    enc_ffn_sum = reduction("enc_ffn", enc_ffn_grads, ffn_layout, ffn_outs)
+    reg_ffn.total()
+    reg_attn.deal()
+    patch_grad, _, *enc_attn_grads = binned_call(
         functools.partial(enc_attention_kernel, images, parts),
         "enc_attention_grad",
         images,
+        chain,
         meta,
-        cut(enc_grad_mid, x, triple, enc_totals, enc_normed_t, enc_mixed_t) + both(enc_gains, enc_scales),
-        None,
+        cut(enc_grad_mid, x, triple, enc_totals, enc_normed_t, enc_mixed_t)
+        + both(enc_gains, enc_scales, reg_small, reg_attn_small, enc_small, reg_wide_sum, enc_wide_sum),
         (enc_output, enc_project),
         [((size, width), F32)],
-        [((small_rows, width), F32), ((4 * part, width), BF16)],
+        [((small_rows, width), F32)] + [((2 * part + extra, width), BF16)] * 2,
         [
             vm(enc_output.shape),
             vm(enc_project.shape),
@@ -1031,15 +1268,31 @@
             vm((part, 3 * width), F32),
             vm((part, width), F32),
         ],
-        6_000_000_000,
-    )
+    )
+
+    enc_attn = reduction(
+        "enc_attention",
+        enc_attn_grads,
+        ([("rows", 0, part), ("rows", part, part), ("rows", 2 * part, extra)], [("blocks", 0, 2)]),
+        (weight((part, width)), weight((part, width)), weight((extra, width)), weight((part, 2 * width))),
+    )
+    reg_ffn.gather()
+    reg_attn.total()
+    enc_ffn_sum.merge(1)
+    enc_attn.merge(1)
+    reg_attn.gather()
+    enc_ffn_sum.merge(2)
+    enc_attn.merge(2)
+    reg_reduce_grad, reg_expand_grad = reg_ffn.finish()
+    enc_ffn_sum.add()
+    enc_attn.add()
 
     def own_places(places):
         mine = lax.dynamic_slice_in_dim(places, band * band_rows, band_rows, 1)
         return mine[:, :, None]
 
     by_image = pl.BlockSpec((None, band_rows, 1), lambda i, m: (i, 0, 0))
-    bin_of_image = pl.BlockSpec((None, size, width), lambda i, m: (m[2 + i], 0, 0))
+    bin_of_image = pl.BlockSpec((None, size, width), lambda i, m: (m[HEAD + i], 0, 0))
     image_out = pl.BlockSpec((None, band_rows, width), lambda i, m: (i, 0, 0))
     prediction, query_grad, patch_grad = pl.pallas_call(
         unpack_kernel,
@@ -1048,40 +1301,24 @@
         grid_spec=pltpu.PrefetchScalarGridSpec(
             num_scalar_prefetch=1,
             grid=(images,),
-            in_specs=[by_image, by_image, bin_of_image, bin_of_image, bin_of_image],
+            in_specs=[IN_HBM, by_image, by_image, bin_of_image, bin_of_image, bin_of_image],
             out_specs=[image_out] * 3,
         ),
         compiler_params=pltpu.CompilerParams(vmem_limit_bytes=VMEM_LIMIT),
-        cost_estimate=pl.CostEstimate(flops=2_000_000_000, bytes_accessed=20_000_000, transcendentals=0),
-    )(meta, own_places(keep_place), own_places(pick_place), final_rows, query_grad, patch_grad)
-
-    def reduce_batch(grads):
-        return lax.psum(grads, "batch").astype(F32)
-
-    def side_by_side(rows, pieces):
-        return jnp.concatenate(jnp.split(rows, pieces, 0), 1)
-
-    wide_pieces = hidden // width
-    reg_ffn_grads = reduce_batch(reg_ffn_grads)
-    reg_attn_grads = reduce_batch(reg_attn_grads)
-    enc_ffn_grads = reduce_batch(enc_ffn_grads)
-    enc_attn_grads = reduce_batch(enc_attn_grads)
-    reg_reduce_grad = reg_ffn_grads[:part_hidden]
-    reg_expand_grad = side_by_side(reg_ffn_grads[part_hidden:], wide_pieces)
-    reg_query_grad = reg_attn_grads[:part]
-    reg_keyval_grad = side_by_side(reg_attn_grads[part : 3 * part], 2)
-    reg_output_grad = reg_attn_grads[3 * part :]
-    enc_reduce_grad = enc_ffn_grads[:part_hidden]
-    enc_expand_grad = side_by_side(enc_ffn_grads[part_hidden:], wide_pieces)
-    enc_output_grad = enc_attn_grads[:part]
-    enc_project_grad = side_by_side(enc_attn_grads[part:], 3)
-
-    small = jnp.concatenate([reg_small, reg_attn_small, enc_small, enc_attn_small], 0)
-    small = lax.dynamic_slice_in_dim(small, band * part, part, 1)
-    wide = jnp.concatenate([reg_wide_sum[:1], enc_wide_sum[:1]], 0)
-    wide = lax.dynamic_slice_in_dim(wide, band * part_hidden, part_hidden, 1)
-    small, wide = lax.psum((small, wide), "batch")
-    reg_s, reg_a, enc_s, enc_a = jnp.split(small, 4, 0)
+        cost_estimate=LONG,
+    )(meta, chain.last, own_places(keep_place), own_places(pick_place), final_rows, query_grad, patch_grad)
+
+    chain.last = prediction
+    enc_ffn_sum.assemble(2)
+    enc_attn.assemble(2)
+    reg_query_grad, reg_output_grad, reg_keyval_grad = reg_attn.finish()
+    enc_ffn_sum.assemble(1)
+    enc_attn.assemble(1)
+    enc_reduce_grad, enc_expand_grad = enc_ffn_sum.finish()
+    enc_output_grad, project_query, vectors, project_rest = enc_attn.finish()
+    enc_project_grad = jnp.concatenate([project_query, project_rest], 1)
+    reg_s, reg_a, enc_s, enc_a = jnp.split(vectors[: 4 * small_rows, :part], 4, 0)
+    reg_wide_grad, enc_wide_grad = vectors[4 * small_rows], vectors[5 * small_rows]
     enc_gains_grad = jnp.stack([enc_a[3], enc_s[2]])
     enc_shifts_grad = jnp.stack([enc_a[4], enc_a[1], enc_a[2], enc_a[0], enc_s[3], enc_s[1]])
     enc_scales_grad = jnp.stack([enc_s[4], enc_s[0]])
@@ -1096,7 +1333,7 @@
         query_grad,
         enc_gains_grad,
         enc_shifts_grad,
-        wide[1],
+        enc_wide_grad,
         enc_scales_grad,
         enc_project_grad,
         enc_output_grad,
@@ -1104,7 +1341,7 @@
         enc_reduce_grad,
         reg_gains_grad,
         reg_shifts_grad,
-        wide[0],
+        reg_wide_grad,
         reg_scales_grad,
         reg_query_grad,
         reg_keyval_grad,

time: 468 us -> 380 us (0.81)
  waiting for transfers between devices: 247 us -> 94.5 us
  Pallas kernels: 97.3 us -> 186 us
  blocking collectives: 78.8 us -> 6.19 us
  starting transfers between devices: 0.15 us -> 45.6 us
    psum x1 -> x0, waiting for transfers between devices: 182 us -> none  [reduce_batch(): return lax.psum(grads, 'batch').astype(F32)]
    psum x1 -> x0, blocking collectives: 72.7 us -> none  [body(): small, wide = lax.psum((small, wide), 'batch')]
    ppermute x0 -> x28, waiting for transfers between devices: none -> 72.5 us  [exchange(): lax.ppermute(array, 'batch', [(i, i ^ offset) for i in range(self.batch_s...]
    pallas_call x5, Pallas kernels: 85.5 us -> 141 us  [binned_call(): pl.pallas_call(for_used_bins(kernel), name=name, out_shape=out_shape, gri...]
    ppermute x0 -> x28, starting transfers between devices: none -> 45.5 us  [exchange(): lax.ppermute(array, 'batch', [(i, i ^ offset) for i in range(self.batch_s...]
    pallas_call x0 -> x20, Pallas kernels: none -> 30 us  [call(): pl.pallas_call(copied_in, name=self.name + '_' + step, out_shape=out_shap...]
    all_gather x1, waiting for transfers between devices: 30.1 us -> 1.66 us  [body(): grad_rows = lax.all_gather(cotangent, 'band', axis=0)]
    all_gather x2 -> x1, waiting for transfers between devices: 32.5 us -> 19.6 us  [body(): lax.all_gather(jnp.where(masked[:, :, None] == 0, patches, queries), 'ban...]
  transfers between devices with their start and end apart: 4 -> 30, of which waited for: 4 -> 12; matrix products, arithmetic and copies ran while one was open for 2% -> 1% of each run, Pallas kernels for 7% -> 37%
where the time goes in v2:
time: 380 us; the launch traced here: 374 us
  Pallas kernels  186 us (49%)
  waiting for transfers between devices  94.5 us (25%)
  starting transfers between devices  45.6 us (12%)
  local copies, waits for them, and re-layouts  18.3 us (5%)
  between operations  15 us (4%)
  other arithmetic  8.12 us (2%)
  blocking collectives  6.19 us (2%)
    pallas_call x5, Pallas kernels, binned_call(): pl.pallas_call(for_used_bins(kernel), name=name, out_shape=out_shape, gri...  141 us
    ppermute x28, waiting for transfers between devices, exchange(): lax.ppermute(array, 'batch', [(i, i ^ offset) for i in range(self.batch_s...  72.5 us
    ppermute x28, starting transfers between devices, exchange(): lax.ppermute(array, 'batch', [(i, i ^ offset) for i in range(self.batch_s...  45.5 us
    pallas_call x20, Pallas kernels, call(): pl.pallas_call(copied_in, name=self.name + '_' + step, out_shape=out_shap...  30 us
    all_gather x1, waiting for transfers between devices, body(): lax.all_gather(jnp.where(masked[:, :, None] == 0, patches, queries), 'ban...  19.6 us
    unnamed x48, local copies, waits for them, and re-layouts  14.4 us
    pallas_call x1, Pallas kernels, body(): pl.pallas_call(unpack_kernel, name='unpack', out_shape=[jax.ShapeDtypeStr...  12 us
  transfers between devices with their start and end apart: 30, of which 12 were waited for; matrix products, arithmetic and copies ran while one was open for 1% of the time, Pallas kernels for 37%

profile of v2, /device:TPU:0, one launch (start us, length us, event | category | flops | bytes accessed | tf_op | source)
XLA Modules:
  0.0 373.9 jit_solution(2296470521584425569)
XLA Ops:
  11.2 6.2 %all-gather.2 = f32[4,64,8]{1,2,0:T(8,128)S(1)} all-gather(f32[1,64,8]{1,2,0:T(8,128)S(1)} %convert_bitcast_fusion), channel_id=1, replica_groups=mesh['batch'=8,'band'=4] {'band'}, dimensions={0}, use_global_device_ids=true | all-gather | bytes 10240 | tf_op jit(solution)/shard_map/all_gather | solution.py:1042
  22.1 19.6 %all-gather.6.cloned.1.call-done = bf16[32,64,768]{2,1,0:T(8,128)(2,1)} async-done(((bf16[8,64,768]{2,1,0:T(8,128)(2,1)}), bf16[32,64,768]{2,1,0:T(8,128)(2,1)}) %all-gather.6.cloned.1.call-update) | async-done | bytes 3145744 | tf_op jit(solution)/shard_map/all_gather | solution.py:1046
  41.8 28.5 %enc_forward.1 = (bf16[8,256,768]{2,1,0:T(8,128)(2,1)}, bf16[8,256,2304]{2,1,0:T(8,128)(2,1)}, f32[8,256,128]{2,1,0:T(8,128)}, bf16[8,192,256]{2,1,0:T(8,128)(2,...) custom-call(s32[43]{0:T(128)} %get-tuple-element.89.meta_ref, ...), custom_call_target="tpu_custom_call" | custom-call | flops 20000000000 | bytes 10000000 | tf_op jit(solution)/shard_map/enc_forward/pallas_call | solution.py:828
  71.9 45.0 %reg_forward.1 = (bf16[8,256,768]{2,1,0:T(8,128)(2,1)}, bf16[8,256,768]{2,1,0:T(8,128)(2,1)}, f32[8,256,128]{2,1,0:T(8,128)}, bf16[8,192,256]{2,1,0:T(8,128)(2,1...) custom-call(s32[43]{0:T(128)} %get-tuple-element.89.meta_ref, ...), custom_call_target="tpu_custom_call" | custom-call | flops 20000000000 | bytes 10000000 | tf_op jit(solution)/shard_map/reg_forward/pallas_call | solution.py:828
  118.4 25.3 %reg_attention_grad.1 = (f32[8,256,768]{2,1,0:T(8,128)}, f32[8,256,768]{2,1,0:T(8,128)}, f32[8,768]{1,0:T(8,128)}, bf16[384,768]{1,0:T(8,128)(2,1)}, bf16[384,768]{1,0:T(8,128)(2,1)}) custom-call(s32[43]{0:T(128)} %get-tuple-element.89.meta_ref, bf16[768,768]{1,0:T(8,128)(2,1)} %get-tuple-element.93._, bf16[8,256,768]{2,1,0:T(8,128)(2,1)} %get-tuple-element.94.refs_0_, ...), custom_call_target="tpu_custom_call" | custom-call | flops 20000000000 | bytes 10000000 | tf_op jit(solution)/shard_map/reg_attention_grad/pallas_call | solution.py:828
  148.5 3.9 %collective-permute-start.2 = (bf16[192,768]{1,0:T(8,128)(2,1)S(1)}, bf16[192,768]{1,0:T(8,128)(2,1)S(1)}, u32[]{:S(2)}, u32[]{:S(2)}) collective-permute-start(bf16[192,768]{1,0:T(8,128)(2,1)S(1)} %get-tuple-element.113), channel_id=1, source_target_pairs={{0,16},{4,20},{8,24},{12,28},{16,0},{20,4},{24,8},{28,12},{1,17},{... | collective-permute-start | bytes 884744 | tf_op jit(solution)/shard_map/ppermute | solution.py:925
  152.8 19.0 %enc_ffn_grad.1 = (f32[8,256,768]{2,1,0:T(8,128)}, f32[8,768]{1,0:T(8,128)}, f32[8,3072]{1,0:T(8,128)}, bf16[768,768]{1,0:T(8,128)(2,1)}, bf16[768,768]{1,0:T(8,128)(2,1)}) custom-call(s32[43]{0:T(128)} %get-tuple-element.89.meta_ref, bf16[192,768]{1,0:T(8,128)(2,1)} %copy-done.16, f32[8,256,768]{2,1,0:T(8,128)} %get-tuple-element.107.refs_0_, ...), custom_call_target="tpu_custom_call" | custom-call | flops 20000000000 | bytes 10000000 | tf_op jit(solution)/shard_map/enc_ffn_grad/pallas_call | solution.py:828
  175.6 5.0 %collective-permute-start.5 = (bf16[192,768]{1,0:T(8,128)(2,1)S(1)}, bf16[192,768]{1,0:T(8,128)(2,1)S(1)}, u32[]{:S(2)}, u32[]{:S(2)}) collective-permute-start(bf16[192,768]{1,0:T(8,128)(2,1)S(1)} %reg_ffn_total.1._.refs_0_), channel_id=1, source_target_pairs={{0,8},{4,12},{8,0},{12,4},{16,24},{20,28},{24,16},{28,20},{1,9},{5... | collective-permute-start | bytes 884744 | tf_op jit(solution)/shard_map/ppermute | solution.py:925
  185.7 23.3 %enc_attention_grad.1 = (f32[8,256,768]{2,1,0:T(8,128)}, f32[8,768]{1,0:T(8,128)}, bf16[448,768]{1,0:T(8,128)(2,1)}, bf16[448,768]{1,0:T(8,128)(2,1)}) custom-call(s32[43]{0:T(128)} %get-tuple-element.89.meta_ref, bf16[96,768]{1,0:T(8,128)(2,1)} %copy-done.18, f32[8,256,768]{2,1,0:T(8,128)} %get-tuple-element.117.refs_0_, ...), custom_call_target="tpu_custom_call" | custom-call | flops 20000000000 | bytes 10000000 | tf_op jit(solution)/shard_map/enc_attention_grad/pallas_call | solution.py:828
  216.0 4.9 %collective-permute-done.9.refs_2_ = bf16[96,768]{1,0:T(8,128)(2,1)S(1)} collective-permute-done((bf16[96,768]{1,0:T(8,128)(2,1)S(1)}, bf16[96,768]{1,0:T(8,128)(2,1)S(1)}, u32[]{:S(2)}, u32[]{:S(2)}) %collective-permute-start.9) | collective-permute-done | bytes 147488 | tf_op jit(solution)/shard_map/ppermute | solution.py:925
  229.1 3.2 collective-permute-start.14
  237.0 8.8 %collective-permute-done.13.refs_1_ = bf16[96,768]{1,0:T(8,128)(2,1)S(1)} collective-permute-done((bf16[96,768]{1,0:T(8,128)(2,1)S(1)}, bf16[96,768]{1,0:T(8,128)(2,1)S(1)}, u32[]{:S(2)}, u32[]{:S(2)}) %collective-permute-start.13) | collective-permute-done | bytes 147488 | tf_op jit(solution)/shard_map/ppermute | solution.py:925
  247.6 6.3 %collective-permute-done.15.refs_3_ = bf16[96,768]{1,0:T(8,128)(2,1)S(1)} collective-permute-done((bf16[96,768]{1,0:T(8,128)(2,1)S(1)}, bf16[96,768]{1,0:T(8,128)(2,1)S(1)}, u32[]{:S(2)}, u32[]{:S(2)}) %collective-permute-start.15) | collective-permute-done | bytes 147488 | tf_op jit(solution)/shard_map/ppermute | solution.py:925
  258.5 3.2 collective-permute-start.20
  261.7 3.5 reg_ffn_finish.1
  265.3 10.2 %collective-permute-done.19.refs_1_ = bf16[192,768]{1,0:T(8,128)(2,1)S(1)} collective-permute-done((bf16[192,768]{1,0:T(8,128)(2,1)S(1)}, bf16[192,768]{1,0:T(8,128)(2,1)S(1)}, u32[]{:S(2)}, u32[]{:S(2)}) %collective-permute-start.19) | collective-permute-done | bytes 294944 | tf_op jit(solution)/shard_map/ppermute | solution.py:925
  279.9 12.0 %unpack.1 = (f32[8,64,768]{2,1,0:T(8,128)}, f32[8,64,768]{2,1,0:T(8,128)}, f32[8,64,768]{2,1,0:T(8,128)}) custom-call(s32[43]{0:T(128)} %get-tuple-element.89.meta_ref, bf16[112,768]{1,0:T(8,128)(2,1)} %copy-done.3, s32[8,64,1]{2,1,0:T(8,128)} %copy.50.keep_place, s32[8,64,1]{2,1,0:T(8,128)} %copy.51.pick_place, ...), custom_call_target="tpu_custom_call" | custom-call | flops 20000000000 | bytes 10000000 | tf_op jit(solution)/shard_map/unpack/pallas_call | solution.py:1297
  294.3 4.3 %collective-permute-start.22 = (bf16[112,768]{1,0:T(8,128)(2,1)S(1)}, bf16[112,768]{1,0:T(8,128)(2,1)S(1)}, u32[]{:S(2)}, u32[]{:S(2)}) collective-permute-start(bf16[112,768]{1,0:T(8,128)(2,1)S(1)} %copy-done.4), channel_id=1, source_target_pairs={{0,16},{4,20},{8,24},{12,28},{16,0},{20,4},{24,8},{28,12},{1,17},{... | collective-permute-start | bytes 516104 | tf_op jit(solution)/shard_map/ppermute | solution.py:925
  298.6 10.7 %collective-permute-done.22.refs_1_ = bf16[112,768]{1,0:T(8,128)(2,1)S(1)} collective-permute-done((bf16[112,768]{1,0:T(8,128)(2,1)S(1)}, bf16[112,768]{1,0:T(8,128)(2,1)S(1)}, u32[]{:S(2)}, u32[]{:S(2)}) %collective-permute-start.22) | collective-permute-done | bytes 172064 | tf_op jit(solution)/shard_map/ppermute | solution.py:925
  317.2 4.0 %collective-permute-start.25 = (bf16[224,768]{1,0:T(8,128)(2,1)S(1)}, bf16[224,768]{1,0:T(8,128)(2,1)S(1)}, u32[]{:S(2)}, u32[]{:S(2)}) collective-permute-start(bf16[224,768]{1,0:T(8,128)(2,1)S(1)} %enc_attention_assemble2.1._.refs_0_), channel_id=1, source_target_pairs={{0,8},{4,12},{8,0},{12,4},{16,24},{20,28},{24,16},{28,20},{1,9},{5... | collective-permute-start | bytes 1032200 | tf_op jit(solution)/shard_map/ppermute | solution.py:925
  321.2 7.6 %collective-permute-done.25.refs_1_ = bf16[224,768]{1,0:T(8,128)(2,1)S(1)} collective-permute-done((bf16[224,768]{1,0:T(8,128)(2,1)S(1)}, bf16[224,768]{1,0:T(8,128)(2,1)S(1)}, u32[]{:S(2)}, u32[]{:S(2)}) %collective-permute-start.25) | collective-permute-done | bytes 344096 | tf_op jit(solution)/shard_map/ppermute | solution.py:925
  331.4 12.7 %collective-permute-done.26.refs_1_ = bf16[768,768]{1,0:T(8,128)(2,1)S(1)} collective-permute-done((bf16[768,768]{1,0:T(8,128)(2,1)S(1)}, bf16[768,768]{1,0:T(8,128)(2,1)S(1)}, u32[]{:S(2)}, u32[]{:S(2)}) %collective-permute-start.26) | collective-permute-done | bytes 1179680 | tf_op jit(solution)/shard_map/ppermute | solution.py:925
  344.1 3.5 enc_ffn_finish.1
  347.6 9.7 %collective-permute-done.27.refs_1_ = bf16[448,768]{1,0:T(8,128)(2,1)S(1)} collective-permute-done((bf16[448,768]{1,0:T(8,128)(2,1)S(1)}, bf16[448,768]{1,0:T(8,128)(2,1)S(1)}, u32[]{:S(2)}, u32[]{:S(2)}) %collective-permute-start.27) | collective-permute-done | bytes 688160 | tf_op jit(solution)/shard_map/ppermute | solution.py:925
  (138 shorter events, 78.6 us)
Async XLA Ops:
  7.2 34.5 %all-gather.6.cloned.1.call-start = ((), (), s32[]{:S(2)}) async-start(), calls=%async_computation | async-start | bytes 3932160 | tf_op jit(solution)/shard_map/all_gather | solution.py:1046
  10.4 61.5 %all-gather.8.cloned.1.call-start = ((), (), s32[]{:S(2)}) async-start(), calls=%async_computation.1 | async-start | bytes 3932160 | tf_op jit(solution)/shard_map/all_gather | solution.py:1047
  116.9 28.4 %collective-permute-start = (bf16[768,768]{1,0:T(8,128)(2,1)}, bf16[768,768]{1,0:T(8,128)(2,1)S(1)}, u32[]{:S(2)}, u32[]{:S(2)}) collective-permute-start(bf16[768,768]{1,0:T(8,128)(2,1)} %get-tuple-element.93._), channel_id=1, source_target_pairs={{0,4},{4,0},{8,12},{12,8},{16,20},{20,16},{24,28},{28,24},{1,5},{5... | collective-permute-start | bytes 3538952 | tf_op jit(solution)/shard_map/ppermute | solution.py:925
  143.8 39.4 %collective-permute-start.4 = (bf16[384,768]{1,0:T(8,128)(2,1)}, bf16[384,768]{1,0:T(8,128)(2,1)S(1)}, u32[]{:S(2)}, u32[]{:S(2)}) collective-permute-start(bf16[384,768]{1,0:T(8,128)(2,1)} %get-tuple-element.104._), channel_id=1, source_target_pairs={{0,4},{4,0},{8,12},{12,8},{16,20},{20,16},{24,28},{28,24},{1,5},{5... | collective-permute-start | bytes 1769480 | tf_op jit(solution)/shard_map/ppermute | solution.py:925
  148.5 24.9 %collective-permute-start.1 = (bf16[192,768]{1,0:T(8,128)(2,1)S(1)}, bf16[192,768]{1,0:T(8,128)(2,1)S(1)}, u32[]{:S(2)}, u32[]{:S(2)}) collective-permute-start(bf16[192,768]{1,0:T(8,128)(2,1)S(1)} %get-tuple-element.112), channel_id=1, source_target_pairs={{0,8},{4,12},{8,0},{12,4},{16,24},{20,28},{24,16},{28,20},{1,9},{5... | collective-permute-start | bytes 884744 | tf_op jit(solution)/shard_map/ppermute | solution.py:925
  148.5 24.9 %collective-permute-start.2 = (bf16[192,768]{1,0:T(8,128)(2,1)S(1)}, bf16[192,768]{1,0:T(8,128)(2,1)S(1)}, u32[]{:S(2)}, u32[]{:S(2)}) collective-permute-start(bf16[192,768]{1,0:T(8,128)(2,1)S(1)} %get-tuple-element.113), channel_id=1, source_target_pairs={{0,16},{4,20},{8,24},{12,28},{16,0},{20,4},{24,8},{28,12},{1,17},{... | collective-permute-start | bytes 884744 | tf_op jit(solution)/shard_map/ppermute | solution.py:925
  152.3 21.0 %collective-permute-start.3 = (bf16[192,768]{1,0:T(8,128)(2,1)S(1)}, bf16[192,768]{1,0:T(8,128)(2,1)S(1)}, u32[]{:S(2)}, u32[]{:S(2)}) collective-permute-start(bf16[192,768]{1,0:T(8,128)(2,1)S(1)} %get-tuple-element.114), channel_id=1, source_target_pairs={{0,24},{4,28},{8,16},{12,20},{16,8},{20,12},{24,0},{28,4},{1,25},{... | collective-permute-start | bytes 884744 | tf_op jit(solution)/shard_map/ppermute | solution.py:925
  171.8 50.4 %collective-permute-start.11 = (bf16[768,768]{1,0:T(8,128)(2,1)}, bf16[768,768]{1,0:T(8,128)(2,1)S(1)}, u32[]{:S(2)}, u32[]{:S(2)}) collective-permute-start(bf16[768,768]{1,0:T(8,128)(2,1)} %get-tuple-element.111._), channel_id=1, source_target_pairs={{0,4},{4,0},{8,12},{12,8},{16,20},{20,16},{24,28},{28,24},{1,5},{5... | collective-permute-start | bytes 3538952 | tf_op jit(solution)/shard_map/ppermute | solution.py:925
  175.6 33.4 %collective-permute-start.5 = (bf16[192,768]{1,0:T(8,128)(2,1)S(1)}, bf16[192,768]{1,0:T(8,128)(2,1)S(1)}, u32[]{:S(2)}, u32[]{:S(2)}) collective-permute-start(bf16[192,768]{1,0:T(8,128)(2,1)S(1)} %reg_ffn_total.1._.refs_0_), channel_id=1, source_target_pairs={{0,8},{4,12},{8,0},{12,4},{16,24},{20,28},{24,16},{28,20},{1,9},{5... | collective-permute-start | bytes 884744 | tf_op jit(solution)/shard_map/ppermute | solution.py:925
  180.6 30.6 %collective-permute-start.6 = (bf16[192,768]{1,0:T(8,128)(2,1)S(1)}, bf16[192,768]{1,0:T(8,128)(2,1)S(1)}, u32[]{:S(2)}, u32[]{:S(2)}) collective-permute-start(bf16[192,768]{1,0:T(8,128)(2,1)S(1)} %reg_ffn_total.1._.refs_0_), channel_id=1, source_target_pairs={{0,16},{4,20},{8,24},{12,28},{16,0},{20,4},{24,8},{28,12},{1,17},{... | collective-permute-start | bytes 884744 | tf_op jit(solution)/shard_map/ppermute | solution.py:925
  181.8 30.0 %collective-permute-start.7 = (bf16[192,768]{1,0:T(8,128)(2,1)S(1)}, bf16[192,768]{1,0:T(8,128)(2,1)S(1)}, u32[]{:S(2)}, u32[]{:S(2)}) collective-permute-start(bf16[192,768]{1,0:T(8,128)(2,1)S(1)} %reg_ffn_total.1._.refs_0_), channel_id=1, source_target_pairs={{0,24},{4,28},{8,16},{12,20},{16,8},{20,12},{24,0},{28,4},{1,25},{... | collective-permute-start | bytes 884744 | tf_op jit(solution)/shard_map/ppermute | solution.py:925
  184.8 30.2 %collective-permute-start.8 = (bf16[96,768]{1,0:T(8,128)(2,1)S(1)}, bf16[96,768]{1,0:T(8,128)(2,1)S(1)}, u32[]{:S(2)}, u32[]{:S(2)}) collective-permute-start(bf16[96,768]{1,0:T(8,128)(2,1)S(1)} %get-tuple-element.128), channel_id=1, source_target_pairs={{0,8},{4,12},{8,0},{12,4},{16,24},{20,28},{24,16},{28,20},{1,9},{5... | collective-permute-start | bytes 442376 | tf_op jit(solution)/shard_map/ppermute | solution.py:925
  211.8 20.5 %collective-permute-start.12 = (bf16[448,768]{1,0:T(8,128)(2,1)}, bf16[448,768]{1,0:T(8,128)(2,1)S(1)}, u32[]{:S(2)}, u32[]{:S(2)}) collective-permute-start(bf16[448,768]{1,0:T(8,128)(2,1)} %get-tuple-element.127._), channel_id=1, source_target_pairs={{0,4},{4,0},{8,12},{12,8},{16,20},{20,16},{24,28},{28,24},{1,5},{5... | collective-permute-start | bytes 2064392 | tf_op jit(solution)/shard_map/ppermute | solution.py:925
  215.1 46.7 %collective-permute-start.18 = (bf16[768,768]{1,0:T(8,128)(2,1)S(1)}, bf16[768,768]{1,0:T(8,128)(2,1)S(1)}, u32[]{:S(2)}, u32[]{:S(2)}) collective-permute-start(bf16[768,768]{1,0:T(8,128)(2,1)S(1)} %reg_ffn_gather.1._.refs_0_), channel_id=1, source_target_pairs={{0,4},{4,0},{8,12},{12,8},{16,20},{20,16},{24,28},{28,24},{1,5},{5... | collective-permute-start | bytes 3538952 | tf_op jit(solution)/shard_map/ppermute | solution.py:925
  225.2 30.5 %collective-permute-start.16 = (bf16[384,768]{1,0:T(8,128)(2,1)}, bf16[384,768]{1,0:T(8,128)(2,1)}, u32[]{:S(2)}, u32[]{:S(2)}) collective-permute-start(bf16[384,768]{1,0:T(8,128)(2,1)} %get-tuple-element.135), channel_id=1, source_target_pairs={{0,8},{4,12},{8,0},{12,4},{16,24},{20,28},{24,16},{28,20},{1,9},{5... | collective-permute-start | bytes 1769480 | tf_op jit(solution)/shard_map/ppermute | solution.py:925
  229.1 16.7 %collective-permute-start.13 = (bf16[96,768]{1,0:T(8,128)(2,1)S(1)}, bf16[96,768]{1,0:T(8,128)(2,1)S(1)}, u32[]{:S(2)}, u32[]{:S(2)}) collective-permute-start(bf16[96,768]{1,0:T(8,128)(2,1)S(1)} %reg_attention_total.1._.refs_0_), channel_id=1, source_target_pairs={{0,8},{4,12},{8,0},{12,4},{16,24},{20,28},{24,16},{28,20},{1,9},{5... | collective-permute-start | bytes 442376 | tf_op jit(solution)/shard_map/ppermute | solution.py:925
  229.1 18.5 %collective-permute-start.14 = (bf16[96,768]{1,0:T(8,128)(2,1)S(1)}, bf16[96,768]{1,0:T(8,128)(2,1)S(1)}, u32[]{:S(2)}, u32[]{:S(2)}) collective-permute-start(bf16[96,768]{1,0:T(8,128)(2,1)S(1)} %reg_attention_total.1._.refs_0_), channel_id=1, source_target_pairs={{0,16},{4,20},{8,24},{12,28},{16,0},{20,4},{24,8},{28,12},{1,17},{... | collective-permute-start | bytes 442376 | tf_op jit(solution)/shard_map/ppermute | solution.py:925
  232.3 21.6 %collective-permute-start.15 = (bf16[96,768]{1,0:T(8,128)(2,1)S(1)}, bf16[96,768]{1,0:T(8,128)(2,1)S(1)}, u32[]{:S(2)}, u32[]{:S(2)}) collective-permute-start(bf16[96,768]{1,0:T(8,128)(2,1)S(1)} %reg_attention_total.1._.refs_0_), channel_id=1, source_target_pairs={{0,24},{4,28},{8,16},{12,20},{16,8},{20,12},{24,0},{28,4},{1,25},{... | collective-permute-start | bytes 442376 | tf_op jit(solution)/shard_map/ppermute | solution.py:925
  255.3 55.0 %collective-permute-start.23 = (bf16[384,768]{1,0:T(8,128)(2,1)S(1)}, bf16[384,768]{1,0:T(8,128)(2,1)S(1)}, u32[]{:S(2)}, u32[]{:S(2)}) collective-permute-start(bf16[384,768]{1,0:T(8,128)(2,1)S(1)} %reg_attention_gather.1._.refs_0_), channel_id=1, source_target_pairs={{0,4},{4,0},{8,12},{12,8},{16,20},{20,16},{24,28},{28,24},{1,5},{5... | collective-permute-start | bytes 1769480 | tf_op jit(solution)/shard_map/ppermute | solution.py:925
  257.5 17.9 %collective-permute-start.19 = (bf16[192,768]{1,0:T(8,128)(2,1)S(1)}, bf16[192,768]{1,0:T(8,128)(2,1)S(1)}, u32[]{:S(2)}, u32[]{:S(2)}) collective-permute-start(bf16[192,768]{1,0:T(8,128)(2,1)S(1)} %get-tuple-element.140), channel_id=1, source_target_pairs={{0,16},{4,20},{8,24},{12,28},{16,0},{20,4},{24,8},{28,12},{1,17},{... | collective-permute-start | bytes 884744 | tf_op jit(solution)/shard_map/ppermute | solution.py:925
  258.5 19.7 %collective-permute-start.20 = (bf16[112,768]{1,0:T(8,128)(2,1)S(1)}, bf16[112,768]{1,0:T(8,128)(2,1)S(1)}, u32[]{:S(2)}, u32[]{:S(2)}) collective-permute-start(bf16[112,768]{1,0:T(8,128)(2,1)S(1)} %get-tuple-element.141), channel_id=1, source_target_pairs={{0,16},{4,20},{8,24},{12,28},{16,0},{20,4},{24,8},{28,12},{1,17},{... | collective-permute-start | bytes 516104 | tf_op jit(solution)/shard_map/ppermute | solution.py:925
  294.1 18.6 %collective-permute-start.24 = (bf16[384,768]{1,0:T(8,128)(2,1)S(1)}, bf16[384,768]{1,0:T(8,128)(2,1)S(1)}, u32[]{:S(2)}, u32[]{:S(2)}) collective-permute-start(bf16[384,768]{1,0:T(8,128)(2,1)S(1)} %enc_ffn_assemble2.1._.refs_0_), channel_id=1, source_target_pairs={{0,8},{4,12},{8,0},{12,4},{16,24},{20,28},{24,16},{28,20},{1,9},{5... | collective-permute-start | bytes 1769480 | tf_op jit(solution)/shard_map/ppermute | solution.py:925
  314.6 29.4 %collective-permute-start.26 = (bf16[768,768]{1,0:T(8,128)(2,1)S(1)}, bf16[768,768]{1,0:T(8,128)(2,1)S(1)}, u32[]{:S(2)}, u32[]{:S(2)}) collective-permute-start(bf16[768,768]{1,0:T(8,128)(2,1)S(1)} %enc_ffn_assemble1.1._.refs_0_), channel_id=1, source_target_pairs={{0,4},{4,0},{8,12},{12,8},{16,20},{20,16},{24,28},{28,24},{1,5},{5... | collective-permute-start | bytes 3538952 | tf_op jit(solution)/shard_map/ppermute | solution.py:925
  329.7 27.7 %collective-permute-start.27 = (bf16[448,768]{1,0:T(8,128)(2,1)S(1)}, bf16[448,768]{1,0:T(8,128)(2,1)S(1)}, u32[]{:S(2)}, u32[]{:S(2)}) collective-permute-start(bf16[448,768]{1,0:T(8,128)(2,1)S(1)} %enc_attention_assemble1.1._.refs_0_), channel_id=1, source_target_pairs={{0,4},{4,0},{8,12},{12,8},{16,20},{20,16},{24,28},{28,24},{1,5},{5... | collective-permute-start | bytes 2064392 | tf_op jit(solution)/shard_map/ppermute | solution.py:925
  (30 other events, 207.3 us)
Sparse Core Ops, SparseCore 0:
  10.5 31.2 all-gather.5
  43.3 28.5 all-gather.7
